TPU v7x, 256 devices: a whole 4x4x8 slice. The times are simulated.
256 devices in a mesh: seq: 32 (over z, y), chan: 8 (over x, core).
Axes of the slice: x: 4, y: 4, z: 8, core: 2. Of those that a mesh axis runs over, the one named last changes fastest.
Arguments:
- query: bfloat16 [4096, 4096], P('seq', 'chan'), may hold values from -6 to 6
- key: bfloat16 [4096, 4096], P('seq', 'chan'), may hold values from -6 to 6
- value: bfloat16 [4096, 4096], P('seq', 'chan'), may hold values from -6 to 6
- short_taps: float32 [3, 3, 4096], P(None, None, 'chan'), may hold values from -3 to 3
- residue: float32 [4096, 16], P('chan'), may hold values from -6 to 6
- rate: float32 [4096, 16], P('chan'), may hold values from 0.00012207031 to 0.05
- skip: float32 [4096], P('chan'), may hold values from -4 to 4
- out_weight: bfloat16 [4096, 4096], P(None, 'chan'), may hold values from -0.09375 to 0.09375
Outputs:
- mixed: bfloat16 [4096, 4096], P('seq', 'chan')
All inputs are finite; a program needn't handle non-finite values.
Results may differ from a plain program's by a relative error of at most 0.0049.
Values may be sent and summed in bfloat16 or wider, within the bound.
A program may use at most 64 MiB of HBM per device.

v0:
```python
import math

import jax
import jax.numpy as jnp
from jax import lax
from jax.sharding import PartitionSpec as P


def partner(array, axis, distance):
    return lax.ppermute(array, axis, [(i, i ^ 1 << distance) for i in range(lax.axis_size(axis))])


def shifted(value, axis, steps):
    count = lax.axis_size(axis)
    first, last = (max(0, -steps), min(count, count - steps))
    return lax.ppermute(value, axis, [(source, source + steps) for source in range(first, last)])


def short_filter(signal, before, tap_weights):
    length = signal.shape[0]
    joined = jnp.concatenate([before, signal], axis=0).astype(jnp.float32)
    return (
        tap_weights[0] * joined[2:]
        + tap_weights[1] * joined[1 : length + 1]
        + tap_weights[2] * joined[0:length]
    )


def rotate(real_part, imag_part, cos_turn, sin_turn):
    return (
        real_part * cos_turn - imag_part * sin_turn,
        real_part * sin_turn + imag_part * cos_turn,
    )


def transform(real_part, imag_part, cos_table, sin_table, form):
    highest = lax.Precision.HIGHEST
    out_real = jnp.einsum(form, real_part, cos_table, precision=highest) - jnp.einsum(
        form, imag_part, sin_table, precision=highest
    )
    out_imag = jnp.einsum(form, real_part, sin_table, precision=highest) + jnp.einsum(
        form, imag_part, cos_table, precision=highest
    )
    return (out_real, out_imag)


def spectrum(signed_freq, fft_length, mode_rates, residues, row_shape):
    phase_angle = signed_freq.astype(jnp.float32) * (2.0 * math.pi / fft_length)
    half_sine = jnp.sin(0.5 * phase_angle)
    full_sine = jnp.sin(phase_angle)
    odd_freq = (signed_freq % 2).astype(jnp.float32)
    seq_span = float(fft_length // 2)

    def add_mode(mode_index, partial_value):
        sum_real, sum_imag = partial_value
        mode_rate = jnp.reshape(mode_rates[mode_index], row_shape)
        weight = -jnp.reshape(residues[mode_index], row_shape) * jnp.expm1(-mode_rate)
        numerator = weight * (
            odd_freq * (1.0 + jnp.exp(-mode_rate * seq_span))
            - (1.0 - odd_freq) * jnp.expm1(-mode_rate * seq_span)
        )
        keep_factor = jnp.exp(-mode_rate)
        denom_real = -jnp.expm1(-mode_rate) + 2.0 * keep_factor * half_sine * half_sine
        denom_imag = keep_factor * full_sine
        scale_factor = numerator / (denom_real * denom_real + denom_imag * denom_imag)
        return (sum_real + scale_factor * denom_real, sum_imag - scale_factor * denom_imag)

    zero_field = jnp.zeros(row_shape, jnp.float32) + jnp.zeros_like(phase_angle)
    return lax.fori_loop(0, mode_rates.shape[0], add_mode, (zero_field, zero_field))


def dft_tables(cell_index, modulus, sign):
    angle_table = (
        sign
        * 2.0
        * math.pi
        / modulus
        * (cell_index[:, None] * cell_index[None, :] % modulus).astype(jnp.float32)
    )
    return (jnp.cos(angle_table), jnp.sin(angle_table))


def cross_forward(real_part, imag_part, seq_index, seq_count):
    levels = seq_count.bit_length() - 1
    for section_bit in reversed(range(levels)):
        partner_real, partner_imag = partner((real_part, imag_part), "seq", section_bit)
        half_span = 2**section_bit
        upper_side = seq_index // half_span % 2 == 1
        turn_angle = (seq_index % half_span).astype(jnp.float32) * (-math.pi / half_span)
        diff_real, diff_imag = rotate(
            partner_real - real_part,
            partner_imag - imag_part,
            jnp.cos(turn_angle),
            jnp.sin(turn_angle),
        )
        real_part = jnp.where(upper_side, diff_real, real_part + partner_real)
        imag_part = jnp.where(upper_side, diff_imag, imag_part + partner_imag)
    return (real_part, imag_part)


def cross_inverse(real_part, imag_part, seq_index, seq_count):
    levels = seq_count.bit_length() - 1
    for section_bit in range(levels):
        partner_real, partner_imag = partner((real_part, imag_part), "seq", section_bit)
        half_span = 2**section_bit
        upper_side = seq_index // half_span % 2 == 1
        turn_angle = (seq_index % half_span).astype(jnp.float32) * (math.pi / half_span)
        moved_real, moved_imag = rotate(
            jnp.where(upper_side, real_part, partner_real),
            jnp.where(upper_side, imag_part, partner_imag),
            jnp.cos(turn_angle),
            jnp.sin(turn_angle),
        )
        stay_real = jnp.where(upper_side, partner_real, real_part)
        stay_imag = jnp.where(upper_side, partner_imag, imag_part)
        real_part = jnp.where(upper_side, stay_real - moved_real, stay_real + moved_real)
        imag_part = jnp.where(upper_side, stay_imag - moved_imag, stay_imag + moved_imag)
    return (real_part, imag_part)


def signed_frequency(frequency, fft_length):
    return jnp.where(frequency * 2 >= fft_length, frequency - fft_length, frequency)


def spectral_butterfly(gated, residue, rate):
    seq_count = lax.axis_size("seq")
    seq_index = lax.axis_index("seq")
    length, chan_width = gated.shape
    fft_length = 2 * seq_count * length
    base_angle = seq_index.astype(jnp.float32) * (math.pi / seq_count)
    real_part = jnp.stack([gated, gated * jnp.cos(base_angle)])
    imag_part = jnp.stack([jnp.zeros_like(gated), -gated * jnp.sin(base_angle)])
    real_part, imag_part = cross_forward(real_part, imag_part, seq_index, seq_count)
    levels = seq_count.bit_length() - 1
    flipped = jnp.zeros((), jnp.int32)
    for section_bit in range(levels):
        flipped = flipped + seq_index // 2**section_bit % 2 * 2 ** (levels - 1 - section_bit)
    freq_rows = 2 * flipped + jnp.arange(2, dtype=jnp.int32)
    cell_index = jnp.arange(length, dtype=jnp.int32)
    twiddle = (
        -2.0
        * math.pi
        / fft_length
        * (freq_rows[:, None] * cell_index[None, :] % fft_length).astype(jnp.float32)
    )
    cos_twiddle = jnp.cos(twiddle)[:, :, None]
    sin_twiddle = jnp.sin(twiddle)[:, :, None]
    real_part, imag_part = rotate(real_part, imag_part, cos_twiddle, sin_twiddle)
    cos_table, sin_table = dft_tables(cell_index, length, -1.0)
    real_part, imag_part = transform(real_part, imag_part, cos_table, sin_table, "esc,sp->epc")
    frequency = freq_rows[:, None] + 2 * seq_count * cell_index[None, :]
    filter_real, filter_imag = spectrum(
        signed_frequency(frequency, fft_length)[:, :, None],
        fft_length,
        rate.T,
        residue.T,
        (1, 1, chan_width),
    )
    real_part, imag_part = (
        real_part * filter_real - imag_part * filter_imag,
        real_part * filter_imag + imag_part * filter_real,
    )
    real_part, imag_part = transform(real_part, imag_part, cos_table, -sin_table, "epc,ps->esc")
    real_part, imag_part = rotate(real_part, imag_part, cos_twiddle, -sin_twiddle)
    real_part, imag_part = cross_inverse(real_part, imag_part, seq_index, seq_count)
    return (
        real_part[0] + real_part[1] * jnp.cos(base_angle) - imag_part[1] * jnp.sin(base_angle)
    ) / fft_length


def per_device(query, key, value, short_taps, residue, rate, skip, out_weight):
    stacked = jnp.stack([query[-2:], key[-2:], value[-2:]])
    before = shifted(stacked, "seq", 1)
    query_conv = short_filter(query, before[0], short_taps[0])
    key_conv = short_filter(key, before[1], short_taps[1])
    value_conv = short_filter(value, before[2], short_taps[2])
    gated = key_conv * value_conv
    convolved = spectral_butterfly(gated, residue, rate)
    hidden = (query_conv * (convolved + skip * gated)).astype(jnp.bfloat16)
    mixed = jnp.dot(
        lax.all_gather(hidden, "chan", axis=1, tiled=True),
        out_weight,
        preferred_element_type=jnp.float32,
    )
    return mixed.astype(jnp.bfloat16)


def solution(mesh):
    placed = (
        P("seq", "chan"),
        P("seq", "chan"),
        P("seq", "chan"),
        P(None, None, "chan"),
        P("chan", None),
        P("chan", None),
        P("chan"),
        P(None, "chan"),
    )
    return jax.shard_map(
        per_device, mesh=mesh, in_specs=placed, out_specs=P("seq", "chan"), check_vma=False
    )
```

profile of v0, /device:TPU:225, one launch (start us, length us, event | category | flops | bytes accessed | tf_op | source)
XLA Modules:
  0.0 421.3 jit_solution(6443445236745383676)
XLA Ops:
  8.0 3.2 collective-permute-start
  11.2 0.9 fusion.101
  12.2 2.2 collective-permute-done
  14.5 0.9 maximum_convert_fusion.2
  15.4 0.9 maximum_convert_fusion.1
  16.6 1.2 collective-permute-start.1
  17.9 4.3 %collective-permute-start.2 = (f32[2,128,512]{2,1,0:T(8,128)S(1)}, f32[2,128,512]{2,1,0:T(8,128)S(1)}, u32[]{:S(2)}, u32[]{:S(2)}) collective-permute-start(f32[2,128,512]{2,1,0:T(8,128)S(1)} %stack.35), channel_id=1, source_target_pairs={{0,128},{8,136},{16,144},{24,152},{32,160},{40,168},{48,176},{56,1... | collective-permute-start | bytes 1572872 | tf_op jit(solution)/shard_map/ppermute | solution.py:10
  22.4 17.9 %collective-permute-done.1 = f32[2,128,512]{2,1,0:T(8,128)S(1)} collective-permute-done((f32[2,128,512]{2,1,0:T(8,128)S(1)}, f32[2,128,512]{2,1,0:T(8,128)S(1)}, u32[]{:S(2)}, u32[]{:S(2)}) %collective-permute-start.1) | collective-permute-done | bytes 524320 | tf_op jit(solution)/shard_map/ppermute | solution.py:10
  40.3 18.0 %collective-permute-done.2 = f32[2,128,512]{2,1,0:T(8,128)S(1)} collective-permute-done((f32[2,128,512]{2,1,0:T(8,128)S(1)}, f32[2,128,512]{2,1,0:T(8,128)S(1)}, u32[]{:S(2)}, u32[]{:S(2)}) %collective-permute-start.2) | collective-permute-done | bytes 524320 | tf_op jit(solution)/shard_map/ppermute | solution.py:10
  58.5 9.2 %collective-permute-start.3 = (f32[2,128,512]{2,1,0:T(8,128)S(1)}, f32[2,128,512]{2,1,0:T(8,128)S(1)}, u32[]{:S(2)}, u32[]{:S(2)}) collective-permute-start(f32[2,128,512]{2,1,0:T(8,128)S(1)} %get-tuple-element.281), channel_id=1, source_target_pairs={{0,64},{8,72},{16,80},{24,88},{32,96},{40,104},{48,112},{56,120},{... | collective-permute-start | bytes 1572872 | tf_op jit(solution)/shard_map/ppermute | solution.py:10
  67.9 33.2 %collective-permute-done.3 = f32[2,128,512]{2,1,0:T(8,128)S(1)} collective-permute-done((f32[2,128,512]{2,1,0:T(8,128)S(1)}, f32[2,128,512]{2,1,0:T(8,128)S(1)}, u32[]{:S(2)}, u32[]{:S(2)}) %collective-permute-start.3) | collective-permute-done | bytes 524320 | tf_op jit(solution)/shard_map/ppermute | solution.py:10
  101.1 11.2 %collective-permute-done.4 = f32[2,128,512]{2,1,0:T(8,128)S(1)} collective-permute-done((f32[2,128,512]{2,1,0:T(8,128)S(1)}, f32[2,128,512]{2,1,0:T(8,128)S(1)}, u32[]{:S(2)}, u32[]{:S(2)}) %collective-permute-start.4) | collective-permute-done | bytes 524320 | tf_op jit(solution)/shard_map/ppermute | solution.py:10
  112.7 1.5 collective-permute-start.6
  114.3 9.9 %collective-permute-done.5 = f32[2,128,512]{2,1,0:T(8,128)S(1)} collective-permute-done((f32[2,128,512]{2,1,0:T(8,128)S(1)}, f32[2,128,512]{2,1,0:T(8,128)S(1)}, u32[]{:S(2)}, u32[]{:S(2)}) %collective-permute-start.5) | collective-permute-done | bytes 524320 | tf_op jit(solution)/shard_map/ppermute | solution.py:10
  124.2 11.2 %collective-permute-done.6 = f32[2,128,512]{2,1,0:T(8,128)S(1)} collective-permute-done((f32[2,128,512]{2,1,0:T(8,128)S(1)}, f32[2,128,512]{2,1,0:T(8,128)S(1)}, u32[]{:S(2)}, u32[]{:S(2)}) %collective-permute-start.6) | collective-permute-done | bytes 524320 | tf_op jit(solution)/shard_map/ppermute | solution.py:10
  135.8 3.0 collective-permute-start.8
  139.0 8.9 %collective-permute-done.7 = f32[2,128,512]{2,1,0:T(8,128)S(1)} collective-permute-done((f32[2,128,512]{2,1,0:T(8,128)S(1)}, f32[2,128,512]{2,1,0:T(8,128)S(1)}, u32[]{:S(2)}, u32[]{:S(2)}) %collective-permute-start.7) | collective-permute-done | bytes 524320 | tf_op jit(solution)/shard_map/ppermute | solution.py:10
  148.7 10.5 %collective-permute-done.8 = f32[2,128,512]{2,1,0:T(8,128)} collective-permute-done((f32[2,128,512]{2,1,0:T(8,128)S(1)}, f32[2,128,512]{2,1,0:T(8,128)}, u32[]{:S(2)}, u32[]{:S(2)}) %collective-permute-start.8) | collective-permute-done | bytes 524320 | tf_op jit(solution)/shard_map/ppermute | solution.py:10
  159.2 1.5 add_select_fusion.12
  160.7 3.9 collective-permute-start.9
  164.9 25.2 %while.18 = (s32[]{:T(128)}, f32[2,128,512]{2,1,0:T(8,128)S(1)}, f32[2,128,512]{2,1,0:T(8,128)S(1)}, f32[16,512]{1,0:T(8,128)}, f32[16,512]{1,0:T(8,128)}, /*ind...) while((s32[]{:T(128)}, f32[2,128,512]{2,1,0:T(8,128)S(1)}, ...), condition=%wide.region_1.2_spmd.clone.clone.clone, body=%wide.region_0.1_spmd.clone.clone.clone.sunk | while | flops 2373891 | bytes 2137739 | solution.py:69
  190.5 0.9 fusion.33
  191.4 0.9 fusion.32
  192.3 0.9 fusion.16
  193.2 1.1 multiply_add_fusion.2
  194.3 0.8 fusion.43
  195.1 0.8 fusion.37
  196.0 0.8 fusion.14
  196.8 1.0 multiply_add_fusion.1
  197.8 1.3 collective-permute-start.12
  199.4 9.3 %collective-permute-done.12 = f32[2,128,512]{2,1,0:T(8,128)S(1)} collective-permute-done((f32[2,128,512]{2,1,0:T(8,128)S(1)}, f32[2,128,512]{2,1,0:T(8,128)S(1)}, u32[]{:S(2)}, u32[]{:S(2)}) %collective-permute-start.12) | collective-permute-done | bytes 524320 | tf_op jit(solution)/shard_map/ppermute | solution.py:10
  208.6 11.2 %collective-permute-done.11 = f32[2,128,512]{2,1,0:T(8,128)S(1)} collective-permute-done((f32[2,128,512]{2,1,0:T(8,128)S(1)}, f32[2,128,512]{2,1,0:T(8,128)S(1)}, u32[]{:S(2)}, u32[]{:S(2)}) %collective-permute-start.11) | collective-permute-done | bytes 524320 | tf_op jit(solution)/shard_map/ppermute | solution.py:10
  220.1 3.1 collective-permute-start.14
  223.5 10.8 %collective-permute-done.14 = f32[2,128,512]{2,1,0:T(8,128)S(1)} collective-permute-done((f32[2,128,512]{2,1,0:T(8,128)S(1)}, f32[2,128,512]{2,1,0:T(8,128)S(1)}, u32[]{:S(2)}, u32[]{:S(2)}) %collective-permute-start.14) | collective-permute-done | bytes 524320 | tf_op jit(solution)/shard_map/ppermute | solution.py:10
  234.3 11.2 %collective-permute-done.13 = f32[2,128,512]{2,1,0:T(8,128)S(1)} collective-permute-done((f32[2,128,512]{2,1,0:T(8,128)S(1)}, f32[2,128,512]{2,1,0:T(8,128)S(1)}, u32[]{:S(2)}, u32[]{:S(2)}) %collective-permute-start.13) | collective-permute-done | bytes 524320 | tf_op jit(solution)/shard_map/ppermute | solution.py:10
  245.8 1.0 collective-permute-start.16
  247.5 8.4 %collective-permute-done.16 = f32[2,128,512]{2,1,0:T(8,128)S(1)} collective-permute-done((f32[2,128,512]{2,1,0:T(8,128)S(1)}, f32[2,128,512]{2,1,0:T(8,128)S(1)}, u32[]{:S(2)}, u32[]{:S(2)}) %collective-permute-start.16) | collective-permute-done | bytes 524320 | tf_op jit(solution)/shard_map/ppermute | solution.py:10
  255.9 11.2 %collective-permute-done.15 = f32[2,128,512]{2,1,0:T(8,128)S(1)} collective-permute-done((f32[2,128,512]{2,1,0:T(8,128)S(1)}, f32[2,128,512]{2,1,0:T(8,128)S(1)}, u32[]{:S(2)}, u32[]{:S(2)}) %collective-permute-start.15) | collective-permute-done | bytes 524320 | tf_op jit(solution)/shard_map/ppermute | solution.py:10
  267.7 2.4 collective-permute-start.17
  270.2 33.6 %collective-permute-done.18 = f32[2,128,512]{2,1,0:T(8,128)S(1)} collective-permute-done((f32[2,128,512]{2,1,0:T(8,128)S(1)}, f32[2,128,512]{2,1,0:T(8,128)S(1)}, u32[]{:S(2)}, u32[]{:S(2)}) %collective-permute-start.18) | collective-permute-done | bytes 524320 | tf_op jit(solution)/shard_map/ppermute | solution.py:10
  303.8 11.2 %collective-permute-done.17 = f32[2,128,512]{2,1,0:T(8,128)S(1)} collective-permute-done((f32[2,128,512]{2,1,0:T(8,128)S(1)}, f32[2,128,512]{2,1,0:T(8,128)S(1)}, u32[]{:S(2)}, u32[]{:S(2)}) %collective-permute-start.17) | collective-permute-done | bytes 524320 | tf_op jit(solution)/shard_map/ppermute | solution.py:10
  315.3 3.6 collective-permute-start.19
  319.0 1.8 collective-permute-start.20
  321.0 34.1 %collective-permute-done.19 = f32[2,128,512]{2,1,0:T(8,128)S(1)} collective-permute-done((f32[2,128,512]{2,1,0:T(8,128)S(1)}, f32[2,128,512]{2,1,0:T(8,128)S(1)}, u32[]{:S(2)}, u32[]{:S(2)}) %collective-permute-start.19) | collective-permute-done | bytes 524320 | tf_op jit(solution)/shard_map/ppermute | solution.py:10
  355.1 11.2 %collective-permute-done.20 = f32[2,128,512]{2,1,0:T(8,128)S(1)} collective-permute-done((f32[2,128,512]{2,1,0:T(8,128)S(1)}, f32[2,128,512]{2,1,0:T(8,128)S(1)}, u32[]{:S(2)}, u32[]{:S(2)}) %collective-permute-start.20) | collective-permute-done | bytes 524320 | tf_op jit(solution)/shard_map/ppermute | solution.py:10
  366.6 1.6 fusion.24
  368.3 42.3 %all-gather.2.cloned.1.call-done = bf16[128,4096]{1,0:T(8,128)(2,1)} async-done(((bf16[128,512]{1,0:T(8,128)(2,1)}), bf16[128,4096]{1,0:T(8,128)(2,1)}) %all-gather.2.cloned.1.call-update) | async-done | bytes 1048592 | tf_op jit(solution)/shard_map/all_gather | solution.py:181
  410.6 3.9 convolution_convert_fusion
  (135 shorter events, 31.4 us)
Async XLA Ops:
  6.5 404.1 %all-gather.2.cloned.1.call-start = ((), (), s32[]{:S(2)}) async-start(), calls=%async_computation | async-start | bytes 1179648 | tf_op jit(solution)/shard_map/all_gather | solution.py:181
  8.0 6.5 %collective-permute-start = (bf16[3,2,512]{2,1,0:T(2,128)(2,1)S(1)}, bf16[3,2,512]{2,1,0:T(2,128)(2,1)S(1)}, u32[]{:S(2)}, u32[]{:S(2)}) collective-permute-start(bf16[3,2,512]{2,1,0:T(2,128)(2,1)S(1)} %pad_maximum_fusion.1), channel_id=1, source_target_pairs={{0,8},{8,16},{16,24},{24,32},{32,40},{40,48},{48,56},{56,64},{64,7... | collective-permute-start | bytes 18440 | tf_op jit(solution)/shard_map/ppermute | solution.py:16
  16.6 23.7 %collective-permute-start.1 = (f32[2,128,512]{2,1,0:T(8,128)S(1)}, f32[2,128,512]{2,1,0:T(8,128)S(1)}, u32[]{:S(2)}, u32[]{:S(2)}) collective-permute-start(f32[2,128,512]{2,1,0:T(8,128)S(1)} %pad_maximum_fusion), channel_id=1, source_target_pairs={{0,128},{8,136},{16,144},{24,152},{32,160},{40,168},{48,176},{56,1... | collective-permute-start | bytes 1572872 | tf_op jit(solution)/shard_map/ppermute | solution.py:10
  17.9 40.3 %collective-permute-start.2 = (f32[2,128,512]{2,1,0:T(8,128)S(1)}, f32[2,128,512]{2,1,0:T(8,128)S(1)}, u32[]{:S(2)}, u32[]{:S(2)}) collective-permute-start(f32[2,128,512]{2,1,0:T(8,128)S(1)} %stack.35), channel_id=1, source_target_pairs={{0,128},{8,136},{16,144},{24,152},{32,160},{40,168},{48,176},{56,1... | collective-permute-start | bytes 1572872 | tf_op jit(solution)/shard_map/ppermute | solution.py:10
  58.5 42.6 %collective-permute-start.3 = (f32[2,128,512]{2,1,0:T(8,128)S(1)}, f32[2,128,512]{2,1,0:T(8,128)S(1)}, u32[]{:S(2)}, u32[]{:S(2)}) collective-permute-start(f32[2,128,512]{2,1,0:T(8,128)S(1)} %get-tuple-element.281), channel_id=1, source_target_pairs={{0,64},{8,72},{16,80},{24,88},{32,96},{40,104},{48,112},{56,120},{... | collective-permute-start | bytes 1572872 | tf_op jit(solution)/shard_map/ppermute | solution.py:10
  67.7 44.7 %collective-permute-start.4 = (f32[2,128,512]{2,1,0:T(8,128)S(1)}, f32[2,128,512]{2,1,0:T(8,128)S(1)}, u32[]{:S(2)}, u32[]{:S(2)}) collective-permute-start(f32[2,128,512]{2,1,0:T(8,128)S(1)} %get-tuple-element.282), channel_id=1, source_target_pairs={{0,64},{8,72},{16,80},{24,88},{32,96},{40,104},{48,112},{56,120},{... | collective-permute-start | bytes 1572872 | tf_op jit(solution)/shard_map/ppermute | solution.py:10
  112.6 11.6 %collective-permute-start.5 = (f32[2,128,512]{2,1,0:T(8,128)S(1)}, f32[2,128,512]{2,1,0:T(8,128)S(1)}, u32[]{:S(2)}, u32[]{:S(2)}) collective-permute-start(f32[2,128,512]{2,1,0:T(8,128)S(1)} %get-tuple-element.279), channel_id=1, source_target_pairs={{0,32},{8,40},{16,48},{24,56},{32,0},{40,8},{48,16},{56,24},{64,96... | collective-permute-start | bytes 1572872 | tf_op jit(solution)/shard_map/ppermute | solution.py:10
  112.7 22.7 %collective-permute-start.6 = (f32[2,128,512]{2,1,0:T(8,128)S(1)}, f32[2,128,512]{2,1,0:T(8,128)S(1)}, u32[]{:S(2)}, u32[]{:S(2)}) collective-permute-start(f32[2,128,512]{2,1,0:T(8,128)S(1)} %get-tuple-element.280), channel_id=1, source_target_pairs={{0,32},{8,40},{16,48},{24,56},{32,0},{40,8},{48,16},{56,24},{64,96... | collective-permute-start | bytes 1572872 | tf_op jit(solution)/shard_map/ppermute | solution.py:10
  135.7 12.2 %collective-permute-start.7 = (f32[2,128,512]{2,1,0:T(8,128)S(1)}, f32[2,128,512]{2,1,0:T(8,128)S(1)}, u32[]{:S(2)}, u32[]{:S(2)}) collective-permute-start(f32[2,128,512]{2,1,0:T(8,128)S(1)} %get-tuple-element.277), channel_id=1, source_target_pairs={{0,16},{8,24},{16,0},{24,8},{32,48},{40,56},{48,32},{56,40},{64,80... | collective-permute-start | bytes 1572872 | tf_op jit(solution)/shard_map/ppermute | solution.py:10
  135.8 23.4 %collective-permute-start.8 = (f32[2,128,512]{2,1,0:T(8,128)S(1)}, f32[2,128,512]{2,1,0:T(8,128)}, u32[]{:S(2)}, u32[]{:S(2)}) collective-permute-start(f32[2,128,512]{2,1,0:T(8,128)S(1)} %get-tuple-element.278), channel_id=1, source_target_pairs={{0,16},{8,24},{16,0},{24,8},{32,48},{40,56},{48,32},{56,40},{64,80... | collective-permute-start | bytes 1572872 | tf_op jit(solution)/shard_map/ppermute | solution.py:10
  147.9 0.8 copy-start
  160.7 29.5 %collective-permute-start.9 = (f32[2,128,512]{2,1,0:T(8,128)S(1)}, f32[2,128,512]{2,1,0:T(8,128)S(1)}, u32[]{:S(2)}, u32[]{:S(2)}) collective-permute-start(f32[2,128,512]{2,1,0:T(8,128)S(1)} %get-tuple-element.275), channel_id=1, source_target_pairs={{0,8},{8,0},{16,24},{24,16},{32,40},{40,32},{48,56},{56,48},{64,72... | collective-permute-start | bytes 1572872 | tf_op jit(solution)/shard_map/ppermute | solution.py:10
  164.6 25.6 %collective-permute-start.10 = (f32[2,128,512]{2,1,0:T(8,128)S(1)}, f32[2,128,512]{2,1,0:T(8,128)S(1)}, u32[]{:S(2)}, u32[]{:S(2)}) collective-permute-start(f32[2,128,512]{2,1,0:T(8,128)S(1)} %get-tuple-element.276), channel_id=1, source_target_pairs={{0,8},{8,0},{16,24},{24,16},{32,40},{40,32},{48,56},{56,48},{64,72... | collective-permute-start | bytes 1572872 | tf_op jit(solution)/shard_map/ppermute | solution.py:10
  197.8 10.8 %collective-permute-start.12 = (f32[2,128,512]{2,1,0:T(8,128)S(1)}, f32[2,128,512]{2,1,0:T(8,128)S(1)}, u32[]{:S(2)}, u32[]{:S(2)}) collective-permute-start(f32[2,128,512]{2,1,0:T(8,128)S(1)} %get-tuple-element.283), channel_id=1, source_target_pairs={{0,8},{8,0},{16,24},{24,16},{32,40},{40,32},{48,56},{56,48},{64,72... | collective-permute-start | bytes 1572872 | tf_op jit(solution)/shard_map/ppermute | solution.py:10
  199.1 20.8 %collective-permute-start.11 = (f32[2,128,512]{2,1,0:T(8,128)S(1)}, f32[2,128,512]{2,1,0:T(8,128)S(1)}, u32[]{:S(2)}, u32[]{:S(2)}) collective-permute-start(f32[2,128,512]{2,1,0:T(8,128)S(1)} %get-tuple-element.284), channel_id=1, source_target_pairs={{0,8},{8,0},{16,24},{24,16},{32,40},{40,32},{48,56},{56,48},{64,72... | collective-permute-start | bytes 1572872 | tf_op jit(solution)/shard_map/ppermute | solution.py:10
  220.1 14.1 %collective-permute-start.14 = (f32[2,128,512]{2,1,0:T(8,128)S(1)}, f32[2,128,512]{2,1,0:T(8,128)S(1)}, u32[]{:S(2)}, u32[]{:S(2)}) collective-permute-start(f32[2,128,512]{2,1,0:T(8,128)S(1)} %get-tuple-element.269), channel_id=1, source_target_pairs={{0,16},{8,24},{16,0},{24,8},{32,48},{40,56},{48,32},{56,40},{64,80... | collective-permute-start | bytes 1572872 | tf_op jit(solution)/shard_map/ppermute | solution.py:10
  223.2 22.3 %collective-permute-start.13 = (f32[2,128,512]{2,1,0:T(8,128)S(1)}, f32[2,128,512]{2,1,0:T(8,128)S(1)}, u32[]{:S(2)}, u32[]{:S(2)}) collective-permute-start(f32[2,128,512]{2,1,0:T(8,128)S(1)} %get-tuple-element.270), channel_id=1, source_target_pairs={{0,16},{8,24},{16,0},{24,8},{32,48},{40,56},{48,32},{56,40},{64,80... | collective-permute-start | bytes 1572872 | tf_op jit(solution)/shard_map/ppermute | solution.py:10
  223.5 97.5 %copy-start.1 = (bf16[128,512]{1,0:T(8,128)(2,1)S(1)}, bf16[128,512]{1,0:T(8,128)(2,1)}, u32[]{:S(2)}) copy-start(bf16[128,512]{1,0:T(8,128)(2,1)} %param.10) | copy-start | bytes 393220
  245.8 10.1 %collective-permute-start.16 = (f32[2,128,512]{2,1,0:T(8,128)S(1)}, f32[2,128,512]{2,1,0:T(8,128)S(1)}, u32[]{:S(2)}, u32[]{:S(2)}) collective-permute-start(f32[2,128,512]{2,1,0:T(8,128)S(1)} %get-tuple-element.267), channel_id=1, source_target_pairs={{0,32},{8,40},{16,48},{24,56},{32,0},{40,8},{48,16},{56,24},{64,96... | collective-permute-start | bytes 1572872 | tf_op jit(solution)/shard_map/ppermute | solution.py:10
  246.9 20.3 %collective-permute-start.15 = (f32[2,128,512]{2,1,0:T(8,128)S(1)}, f32[2,128,512]{2,1,0:T(8,128)S(1)}, u32[]{:S(2)}, u32[]{:S(2)}) collective-permute-start(f32[2,128,512]{2,1,0:T(8,128)S(1)} %get-tuple-element.268), channel_id=1, source_target_pairs={{0,32},{8,40},{16,48},{24,56},{32,0},{40,8},{48,16},{56,24},{64,96... | collective-permute-start | bytes 1572872 | tf_op jit(solution)/shard_map/ppermute | solution.py:10
  267.4 36.4 %collective-permute-start.18 = (f32[2,128,512]{2,1,0:T(8,128)S(1)}, f32[2,128,512]{2,1,0:T(8,128)S(1)}, u32[]{:S(2)}, u32[]{:S(2)}) collective-permute-start(f32[2,128,512]{2,1,0:T(8,128)S(1)} %get-tuple-element.265), channel_id=1, source_target_pairs={{0,64},{8,72},{16,80},{24,88},{32,96},{40,104},{48,112},{56,120},{... | collective-permute-start | bytes 1572872 | tf_op jit(solution)/shard_map/ppermute | solution.py:10
  267.7 47.4 %collective-permute-start.17 = (f32[2,128,512]{2,1,0:T(8,128)S(1)}, f32[2,128,512]{2,1,0:T(8,128)S(1)}, u32[]{:S(2)}, u32[]{:S(2)}) collective-permute-start(f32[2,128,512]{2,1,0:T(8,128)S(1)} %get-tuple-element.266), channel_id=1, source_target_pairs={{0,64},{8,72},{16,80},{24,88},{32,96},{40,104},{48,112},{56,120},{... | collective-permute-start | bytes 1572872 | tf_op jit(solution)/shard_map/ppermute | solution.py:10
  315.3 39.8 %collective-permute-start.19 = (f32[2,128,512]{2,1,0:T(8,128)S(1)}, f32[2,128,512]{2,1,0:T(8,128)S(1)}, u32[]{:S(2)}, u32[]{:S(2)}) collective-permute-start(f32[2,128,512]{2,1,0:T(8,128)S(1)} %get-tuple-element.264), channel_id=1, source_target_pairs={{0,128},{8,136},{16,144},{24,152},{32,160},{40,168},{48,176},{56,1... | collective-permute-start | bytes 1572872 | tf_op jit(solution)/shard_map/ppermute | solution.py:10
  319.0 47.4 %collective-permute-start.20 = (f32[2,128,512]{2,1,0:T(8,128)S(1)}, f32[2,128,512]{2,1,0:T(8,128)S(1)}, u32[]{:S(2)}, u32[]{:S(2)}) collective-permute-start(f32[2,128,512]{2,1,0:T(8,128)S(1)} %get-tuple-element.263), channel_id=1, source_target_pairs={{0,128},{8,136},{16,144},{24,152},{32,160},{40,168},{48,176},{56,1... | collective-permute-start | bytes 1572872 | tf_op jit(solution)/shard_map/ppermute | solution.py:10
Sparse Core Ops, SparseCore 0:
  368.4 42.1 all-gather.1
where the time goes:
time: 428 us; the launch traced here: 421 us
  waiting for transfers between devices  318 us (74%)
  starting transfers between devices  41.3 us (10%)
  other arithmetic  32.3 us (8%)
  between operations  15.1 us (4%)
  matrix products  11.1 us (3%)
    ppermute x20, waiting for transfers between devices, partner(): lax.ppermute(array, axis, [(i, i ^ 1 << distance) for i in range(lax.axis...  273 us
    all_gather x1, waiting for transfers between devices, per_device(): lax.all_gather(hidden, 'chan', axis=1, tiled=True)  42.3 us
    ppermute x20, starting transfers between devices, partner(): lax.ppermute(array, axis, [(i, i ^ 1 << distance) for i in range(lax.axis...  38.1 us
    mul x16, other arithmetic, add_mode(): -jnp.reshape(residues[mode_index], row_shape) * jnp.expm1(-mode_rate)  12.3 us
  transfers between devices with their start and end apart: 22, of which 20 were waited for; matrix products, arithmetic and copies ran while one was open for 6% of the time, Pallas kernels for 0%

commit v1 on v0

v1 whole, which is shorter than its diff:
```python
import functools

import jax
import jax.numpy as jnp
from jax import lax
from jax.experimental import pallas as pl
from jax.experimental.pallas import tpu as pltpu
from jax.sharding import PartitionSpec as P

MESH = pl.DeviceIdType.MESH
F32 = jnp.float32
BF16 = jnp.bfloat16
MODES = 16
STEPS = 16
SUBS = 8
ROWS = STEPS * SUBS
LANES = 128
CHIPS = 4
CORES = 2
PIECES = 2


def tree_sum(array):
    while array.shape[0] > 1:
        half = array.shape[0] // 2
        array = array[:half] + array[half:]
    return array[0]


def lagged(block, last, last_but_one):
    one = jnp.concatenate([last[None], block[:-1]], axis=0)
    two = jnp.concatenate([last_but_one[None], one[:-1]], axis=0)
    return one, two


def tapped(taps, which, cols, now, one, two):
    return (
        taps[which, 0:1, cols] * now + taps[which, 1:2, cols] * one + taps[which, 2:3, cols] * two
    )


def kernel(
    zs,
    ys,
    q_hbm,
    k_hbm,
    v_hbm,
    taps_hbm,
    res_hbm,
    rate_hbm,
    skip_hbm,
    w_hbm,
    out_ref,
    q_in,
    k_in,
    v_in,
    taps,
    res,
    rate,
    skip,
    weight,
    rate3,
    decay3,
    gain3,
    xq,
    xk,
    xv,
    gated,
    enter,
    power,
    local,
    query,
    msg,
    ring_y,
    edge,
    halo_out,
    halo_in,
    total,
    ring_z,
    before,
    starts,
    start_in,
    hid,
    acc,
    load_sem,
    p1_send,
    p1_recv,
    halo_sem,
    edge_send,
    edge_recv,
    p2_send,
    p2_recv,
    p3_send,
    p3_recv,
    g_send,
    g_recv,
):
    seq = lax.axis_index("seq")
    chan = lax.axis_index("chan")
    z, y = seq // ys, lax.rem(seq, ys)
    x, core = chan // CORES, lax.rem(chan, CORES)
    width = k_in.shape[1]
    tiles = width // LANES
    count = zs * ys

    loads = [
        pltpu.make_async_copy(src, dst, load_sem.at[i])
        for i, (src, dst) in enumerate(
            [
                (rate_hbm, rate),
                (res_hbm, res),
                (taps_hbm, taps),
                (k_hbm, k_in),
                (v_hbm, v_in),
                (q_hbm, q_in),
                (skip_hbm, skip),
                (w_hbm, weight),
            ]
        )
    ]
    for load in loads:
        load.start()

    def at(zz, yy):
        return zz * ys + yy

    right = lax.rem(x + 1, CHIPS) * CORES + core
    left = lax.rem(x + CHIPS - 1, CHIPS) * CORES + core
    sibling = x * CORES + 1 - core
    z_up = lax.rem(z + 1, zs)
    z_down = lax.rem(z + zs - 1, zs)

    barrier = pltpu.get_barrier_semaphore()

    def greet(s, c):
        pl.semaphore_signal(barrier, inc=1, device_id=(s, c), device_id_type=MESH)

    for e in range(1, ys):
        greet(at(z, lax.rem(y + e, ys)), chan)
    for e in range(1, zs):
        greet(at(lax.rem(z + e, zs), y), chan)
    greet(lax.rem(seq + 1, count), chan)
    greet(lax.rem(seq + count - 1, count), chan)
    greet(at(z_down, ys - 1), chan)
    for c in (right, left, sibling):
        greet(seq, c)

    @pl.when(y == ys - 1)
    def _():
        for e in range(ys):
            greet(at(z_up, e), chan)

    loads[0].wait()
    loads[1].wait()
    r = rate[...]
    series = r * (1.0 - r * (1 / 2) * (1.0 - r * (1 / 3) * (1.0 - r * (1 / 4) * (1.0 - r * (1 / 5) * (1.0 - r * (1 / 6))))))
    gain = res[...] * series
    decay = jnp.exp(-r)
    for m in range(MODES):
        rate3[m] = jnp.broadcast_to(r[m : m + 1], (SUBS, width))
        decay3[m] = jnp.broadcast_to(decay[m : m + 1], (SUBS, width))
        gain3[m] = jnp.broadcast_to(gain[m : m + 1], (SUBS, width))

    row = lax.broadcasted_iota(jnp.int32, (ROWS, ROWS), 0)
    col = lax.broadcasted_iota(jnp.int32, (ROWS, ROWS), 1)
    order = jnp.where(col == (row & 7) * STEPS + (row >> 3), 1.0, 0.0).astype(BF16)
    back = jnp.where(row == (col & 7) * STEPS + (col >> 3), 1.0, 0.0).astype(BF16)

    def arranged(block):
        return jnp.dot(order, block, preferred_element_type=F32).reshape(STEPS, SUBS, width)

    sub = lax.broadcasted_iota(jnp.int32, (SUBS, LANES), 0)
    sub3 = lax.broadcasted_iota(jnp.int32, (MODES, SUBS, LANES), 1)
    first = sub == 0
    subf3 = sub3.astype(F32)

    loads[2].wait()
    loads[3].wait()
    loads[4].wait()
    xk[...] = arranged(k_in[...])
    xv[...] = arranged(v_in[...])

    def lags(block):
        last = jnp.where(first, 0.0, pltpu.roll(block[STEPS - 1], 1, 0))
        last_but_one = jnp.where(first, 0.0, pltpu.roll(block[STEPS - 2], 1, 0))
        return lagged(block, last, last_but_one)

    for l in range(tiles):
        cols = slice(l * LANES, (l + 1) * LANES)
        kb, vb = xk[:, :, cols], xv[:, :, cols]
        g = tapped(taps, 1, cols, kb, *lags(kb)) * tapped(taps, 2, cols, vb, *lags(vb))
        g = jnp.concatenate([jnp.where(first[None], 0.0, g[:2]), g[2:]], axis=0)
        gated[:, :, cols] = g
        a = decay3[:, :, cols]
        state = jnp.broadcast_to(g[0][None], a.shape)
        for j in range(1, STEPS):
            state = state * a + g[j][None]
        step = a
        for _ in range(4):
            step = step * step
        for reach in (1, 2, 4):
            state = state + jnp.where(sub3 >= reach, step, 0.0) * pltpu.roll(state, reach, 1)
            step = step * step
        enter[:, :, cols] = jnp.where(sub3 >= 1, pltpu.roll(state, 1, 1), 0.0)
        for m in range(MODES):
            msg[l, m : m + 1, :] = state[m, SUBS - 1 : SUBS, :]
        for i, block in enumerate((kb, vb)):
            base = MODES + 4 * i
            msg[l, base : base + 1, :] = block[0, 0:1, :]
            msg[l, base + 1 : base + 2, :] = block[1, 0:1, :]
            msg[l, base + 2 : base + 3, :] = block[STEPS - 2, SUBS - 1 : SUBS, :]
            msg[l, base + 3 : base + 4, :] = block[STEPS - 1, SUBS - 1 : SUBS, :]

    pl.semaphore_wait(barrier, 3 + (ys - 1) + (zs - 1) + 3 + jnp.where(y == ys - 1, ys, 0))

    p1 = []
    for e in range(1, ys):
        to = lax.rem(y + e, ys)
        p1.append(
            pltpu.make_async_remote_copy(
                msg.at[to], ring_y.at[y], p1_send.at[e - 1], p1_recv.at[e - 1],
                device_id=(at(z, to), chan), device_id_type=MESH,
            )
        )
    edges = [
        pltpu.make_async_remote_copy(
            msg.at[e, pl.ds(MODES, 8)], edge, edge_send.at[e], edge_recv,
            device_id=(at(z_up, e), chan), device_id_type=MESH,
        )
        for e in range(ys)
    ]

    for copy in p1:
        copy.start()

    @pl.when(y == ys - 1)
    def _():
        for copy in edges:
            copy.start()

    loads[5].wait()
    xq[...] = arranged(q_in[...])
    for i, block in enumerate((xq, xk, xv)):
        halo_out[2 * i : 2 * i + 1, :] = block[STEPS - 2, SUBS - 1 : SUBS, :]
        halo_out[2 * i + 1 : 2 * i + 2, :] = block[STEPS - 1, SUBS - 1 : SUBS, :]
    halo_out[6:8, :] = jnp.zeros((2, width), F32)
    halo = pltpu.make_async_remote_copy(
        halo_out, halo_in, halo_sem.at[0], halo_sem.at[1],
        device_id=(lax.rem(seq + 1, count), chan), device_id_type=MESH,
    )
    halo.start()

    def chunk_start(cols, rows_now, rows_before):
        k0, k1, v0, v1 = rows_now
        k126, k127, v126, v127 = rows_before
        g0 = tapped(taps, 1, cols, k0, k127, k126) * tapped(taps, 2, cols, v0, v127, v126)
        g1 = tapped(taps, 1, cols, k1, k0, k127) * tapped(taps, 2, cols, v1, v0, v127)
        return g0, g1

    mine = pl.ds(pl.multiple_of(y * LANES, LANES), LANES)
    r_mine = rate[:, mine]

    ring_y[y] = msg[y]
    a126 = jnp.exp(-(ROWS - 2.0) * r_mine)
    a127 = jnp.exp(-(ROWS - 1.0) * r_mine)
    a128 = jnp.exp(-float(ROWS) * r_mine)
    for copy in p1:
        copy.wait_recv()
    edges[0].wait_recv()
    ends = [jnp.where(z == 0, 0.0, edge[i : i + 1, :]) for i in (2, 3, 6, 7)]
    states = []
    for e in range(ys):
        now = [ring_y[e, MODES + i : MODES + i + 1, :] for i in (0, 1, 4, 5)]
        g0, g1 = chunk_start(mine, now, ends)
        ends = [ring_y[e, MODES + i : MODES + i + 1, :] for i in (2, 3, 6, 7)]
        states.append(ring_y[e, 0:MODES, :] + a127 * g0 + a126 * g1)
    whole = states[0]
    for e in range(1, ys):
        whole = whole * a128 + states[e]
    total[...] = whole

    p2 = []
    for d in range(1, zs):
        copy = pltpu.make_async_remote_copy(
            total, ring_z.at[d - 1], p2_send.at[d - 1], p2_recv.at[d - 1],
            device_id=(at(lax.rem(z + d, zs), y), chan), device_id_type=MESH,
        )
        p2.append(copy)
        pl.when(z + d < zs)(copy.start)

    halo.wait_recv()
    loads[6].wait()
    for l in range(tiles):
        cols = slice(l * LANES, (l + 1) * LANES)
        ends = [jnp.where(seq == 0, 0.0, halo_in[i : i + 1, cols]) for i in range(6)]
        kb, vb = (xk, xv)
        now = [b[j, 0:1, cols] for b in (kb, vb) for j in (0, 1)]
        g0, g1 = chunk_start(cols, now, ends[2:6])
        g = gated[:, :, cols]
        g = jnp.concatenate(
            [jnp.where(first, g0, g[0])[None], jnp.where(first, g1, g[1])[None], g[2:]], axis=0
        )
        r3, a, w = rate3[:, :, cols], decay3[:, :, cols], gain3[:, :, cols]
        wa = w * a
        pw = jnp.exp(-float(STEPS) * subf3 * r3)
        missing = jnp.where(sub3 >= 1, pw * jnp.exp(2.0 * r3) * (a * g0[None] + g1[None]), 0.0)
        enter[:, :, cols] = wa * (enter[:, :, cols] + missing)
        power[:, :, cols] = wa * pw
        near = w * jnp.exp(-subf3 * r3)
        a8 = a * a
        a8 = a8 * a8
        a8 = a8 * a8
        taps_near = (tree_sum(near), tree_sum(near * a8))
        out = g * skip[0:1, cols]
        for d in range(STEPS):
            tap = taps_near[d // SUBS][d % SUBS : d % SUBS + 1, :]
            add = g[: STEPS - d] * tap[None]
            out = out + add if d == 0 else jnp.concatenate([out[:d], out[d:] + add], axis=0)
        local[:, :, cols] = out
        qb = xq[:, :, cols]
        last = jnp.where(first, ends[1], pltpu.roll(qb[STEPS - 1], 1, 0))
        last_but_one = jnp.where(first, ends[0], pltpu.roll(qb[STEPS - 2], 1, 0))
        query[:, :, cols] = tapped(taps, 0, cols, qb, *lagged(qb, last, last_but_one))

    before[...] = jnp.zeros_like(before)
    for d in range(1, zs):

        @pl.when(z >= d)
        def _():
            p2[d - 1].wait_recv()
            before[...] += jnp.exp(-float(ROWS * ys * (d - 1)) * r_mine) * ring_z[d - 1]

    start = before[...]
    for e in range(ys):
        starts[e] = start
        if e < ys - 1:
            start = start * a128 + states[e]

    p3 = []
    for e in range(1, ys):
        to = lax.rem(y + e, ys)
        copy = pltpu.make_async_remote_copy(
            starts.at[to], start_in.at[y], p3_send.at[e - 1], p3_recv.at[e - 1],
            device_id=(at(z, to), chan), device_id_type=MESH,
        )
        copy.start()
        p3.append(copy)
    start_in[y] = starts[y]
    for copy in p3:
        copy.wait_recv()

    sent = []

    def send(index, slot, piece, to_slot, to):
        copy = pltpu.make_async_remote_copy(
            hid.at[slot, piece], hid.at[to_slot, piece], g_send.at[index], g_recv.at[index],
            device_id=(seq, to), device_id_type=MESH,
        )
        copy.start()
        sent.append(copy)
        return copy

    per = tiles // PIECES
    own_sib, own_right, own_left = {}, {}, {}
    for p in range(PIECES):
        for i in range(per):
            l = p * per + i
            cols = slice(l * LANES, (l + 1) * LANES)
            a = decay3[:, :, cols]
            state = jnp.stack(
                [
                    enter[m, :, cols] + power[m, :, cols] * start_in[l, m : m + 1, :]
                    for m in range(MODES)
                ]
            )
            blocks = []
            for j in range(STEPS):
                blocks.append(query[j, :, cols] * (local[j, :, cols] + tree_sum(state)))
                if j < STEPS - 1:
                    state = state * a
            block = jnp.concatenate(blocks, axis=0)
            hid[0, p, :, i * LANES : (i + 1) * LANES] = block.astype(BF16)
        own_right[p] = send(p, 0, p, 6, right)
        own_sib[p] = send(2 + p, 0, p, 1, sibling)
    for p in (1, 0):
        own_left[p] = send(4 + p, 0, p, 2, left)

    loads[7].wait()
    half = width // PIECES

    def product(slot, piece):
        owner = lax.rem(x + slot // CORES, CHIPS) * CORES + (core if slot % CORES == 0 else 1 - core)
        rows = pl.ds(pl.multiple_of(owner * width + piece * half, half), half)
        return jnp.dot(hid[slot, piece], weight[rows, :], preferred_element_type=F32)

    acc[...] = product(0, 0) + product(0, 1)
    for p in range(PIECES):
        own_sib[p].wait_recv()
        acc[...] += product(1, p)

    own_right[0].wait_recv()
    on_right = send(6, 6, 0, 4, right)
    sib = {(7, 0): send(8, 6, 0, 7, sibling)}
    own_left[1].wait_recv()
    on_left = send(7, 2, 1, 4, left)
    sib[3, 1] = send(9, 2, 1, 3, sibling)
    acc[...] += product(6, 0) + product(2, 1)
    for slot, p in ((7, 0), (3, 1)):
        sib[slot, p].wait_recv()
        acc[...] += product(slot, p)
    own_right[1].wait_recv()
    sib[7, 1] = send(10, 6, 1, 7, sibling)
    own_left[0].wait_recv()
    sib[3, 0] = send(11, 2, 0, 3, sibling)
    acc[...] += product(6, 1) + product(2, 0)
    for slot, p in ((7, 1), (3, 0)):
        sib[slot, p].wait_recv()
        acc[...] += product(slot, p)
    on_right.wait_recv()
    sib[5, 0] = send(12, 4, 0, 5, sibling)
    on_left.wait_recv()
    sib[5, 1] = send(13, 4, 1, 5, sibling)
    acc[...] += product(4, 0) + product(4, 1)
    for p in range(PIECES):
        sib[5, p].wait_recv()
        acc[...] += product(5, p)

    mixed = acc[...].astype(BF16)
    out_ref[...] = jnp.dot(back, mixed, preferred_element_type=F32).astype(BF16)

    for copy in p1 + p3 + sent + [halo]:
        copy.wait_send()
    for d in range(1, zs):
        pl.when(z + d < zs)(p2[d - 1].wait_send)

    @pl.when(y == ys - 1)
    def _():
        for copy in edges:
            copy.wait_send()


def per_device(zs, ys, query, key, value, short_taps, residue, rate, skip, out_weight):
    width = query.shape[1]
    tiles = width // LANES
    table = pltpu.VMEM((MODES, SUBS, width), F32)
    block = pltpu.VMEM((STEPS, SUBS, width), F32)
    dma = pltpu.SemaphoreType.DMA
    scratch = [
        pltpu.VMEM((ROWS, width), BF16),
        pltpu.VMEM((ROWS, width), BF16),
        pltpu.VMEM((ROWS, width), BF16),
        pltpu.VMEM(short_taps.shape, F32),
        pltpu.VMEM((MODES, width), F32),
        pltpu.VMEM((MODES, width), F32),
        pltpu.VMEM((1, width), F32),
        pltpu.VMEM(out_weight.shape, BF16),
        table,
        table,
        table,
        block,
        block,
        block,
        block,
        table,
        table,
        block,
        block,
        pltpu.VMEM((tiles, MODES + 8, LANES), F32),
        pltpu.VMEM((ys, MODES + 8, LANES), F32),
        pltpu.VMEM((8, LANES), F32),
        pltpu.VMEM((8, width), F32),
        pltpu.VMEM((8, width), F32),
        pltpu.VMEM((MODES, LANES), F32),
        pltpu.VMEM((zs - 1, MODES, LANES), F32),
        pltpu.VMEM((MODES, LANES), F32),
        pltpu.VMEM((ys, MODES, LANES), F32),
        pltpu.VMEM((ys, MODES, LANES), F32),
        pltpu.VMEM((CHIPS * CORES, PIECES, ROWS, width // PIECES), BF16),
        pltpu.VMEM((ROWS, width), F32),
        dma((8,)),
        dma((ys - 1,)),
        dma((ys - 1,)),
        dma((2,)),
        dma((ys,)),
        dma,
        dma((zs - 1,)),
        dma((zs - 1,)),
        dma((ys - 1,)),
        dma((ys - 1,)),
        dma((14,)),
        dma((14,)),
    ]
    return pl.pallas_call(
        functools.partial(kernel, zs, ys),
        out_shape=jax.ShapeDtypeStruct((ROWS, width), BF16),
        in_specs=[pl.BlockSpec(memory_space=pl.ANY)] * 8,
        out_specs=pl.BlockSpec(memory_space=pltpu.VMEM),
        scratch_shapes=scratch,
        compiler_params=pltpu.CompilerParams(
            collective_id=0, has_side_effects=True, vmem_limit_bytes=56 * 1024 * 1024
        ),
    )(query, key, value, short_taps, residue.T, rate.T, skip[None, :], out_weight)


def solution(mesh, ys=4):
    placed = (
        P("seq", "chan"),
        P("seq", "chan"),
        P("seq", "chan"),
        P(None, None, "chan"),
        P("chan", None),
        P("chan", None),
        P("chan"),
        P(None, "chan"),
    )
    return jax.shard_map(
        functools.partial(per_device, mesh.shape["seq"] // ys, ys),
        mesh=mesh,
        in_specs=placed,
        out_specs=P("seq", "chan"),
        check_vma=False,
    )
```

time: 428 us -> 30.3 us (0.07)
  the two profiles are of different devices: /device:TPU:225 before, /device:TPU:33 now
where the time goes in v1:
time: 30.3 us; the launch traced here: 30.2 us
  Pallas kernels  28.7 us (95%)
  local copies, waits for them, and re-layouts  1.57 us (5%)
    pallas_call x1, Pallas kernels, per_device(): pl.pallas_call(functools.partial(kernel, zs, ys), out_shape=jax.ShapeDtyp...  28.7 us
    unnamed x1, local copies, waits for them, and re-layouts  1.57 us

profile of v1, /device:TPU:33, one launch (start us, length us, event | category | flops | bytes accessed | tf_op | source)
XLA Modules:
  0.0 30.2 jit_solution(15667519295569742029)
XLA Ops:
  0.0 28.7 %shard_map.82 = bf16[128,512]{1,0:T(8,128)(2,1)} custom-call(bf16[128,512]{1,0:T(8,128)(2,1)} %q_hbm.1, bf16[128,512]{1,0:T(8,128)(2,1)} %k_hbm.1, bf16[128,512]{1,0:T(8,128)(2,1)} %v_hbm.1, f32[3,3,512]{2,1,0:T(4,128)} %taps_hbm.1, f32[16,512]{1,0:T(8,128)} %bitcast.3, f32[16,512]{1,0:T(8,128)} %bitcast.4, f32[1,512]{1,0:T(1,128)} %bitcast.5, ...), custom_call_target="tpu_custom_call" | custom-call | tf_op jit(solution)/shard_map/pallas_call | solution.py:493
  28.7 1.6 %copy.10 = bf16[128,512]{1,0:T(8,128)(2,1)} copy(bf16[128,512]{1,0:T(8,128)(2,1)} %shard_map.82) | data formatting | bytes 262144

commit v2 on v1

v2 whole, which is shorter than its diff:
```python
import functools

import jax
import jax.numpy as jnp
from jax import lax
from jax.experimental import pallas as pl
from jax.experimental.pallas import tpu as pltpu
from jax.sharding import PartitionSpec as P

MESH = pl.DeviceIdType.MESH
F32 = jnp.float32
BF16 = jnp.bfloat16
MODES = 16
STEPS = 16
SUBS = 8
ROWS = STEPS * SUBS
LANES = 128
CHIPS = 4
CORES = 2
PIECES = 2


def tree_sum(array):
    while array.shape[0] > 1:
        half = array.shape[0] // 2
        array = array[:half] + array[half:]
    return array[0]


def lagged(block, last, last_but_one):
    one = jnp.concatenate([last[None], block[:-1]], axis=0)
    two = jnp.concatenate([last_but_one[None], one[:-1]], axis=0)
    return one, two


def tapped(taps, which, cols, now, one, two):
    return (
        taps[which, 0:1, cols] * now + taps[which, 1:2, cols] * one + taps[which, 2:3, cols] * two
    )


def kernel(
    zs,
    ys,
    q_hbm,
    k_hbm,
    v_hbm,
    taps_hbm,
    res_hbm,
    rate_hbm,
    skip_hbm,
    w_hbm,
    out_ref,
    q_in,
    k_in,
    v_in,
    taps,
    res,
    rate,
    skip,
    weight,
    rate3,
    decay3,
    gain3,
    xk,
    xv,
    enter,
    power,
    near,
    local,
    query,
    edge_y,
    edge_z,
    state_y,
    heads,
    starts,
    total,
    ring_z,
    before,
    hit,
    hit_later,
    hid,
    acc,
    load_sem,
    y_send,
    y_recv,
    e_send,
    e_recv,
    z_send,
    z_recv,
    g_send,
    g_recv,
    ready,
    ready_edge,
):
    seq = lax.axis_index("seq")
    chan = lax.axis_index("chan")
    z, y = seq // ys, lax.rem(seq, ys)
    x, core = chan // CORES, lax.rem(chan, CORES)
    width = k_in.shape[1]
    tiles = width // LANES
    last_y = y == ys - 1

    loads = [
        pltpu.make_async_copy(src, dst, load_sem.at[i])
        for i, (src, dst) in enumerate(
            [
                (rate_hbm, rate),
                (res_hbm, res),
                (taps_hbm, taps),
                (k_hbm, k_in),
                (v_hbm, v_in),
                (q_hbm, q_in),
                (skip_hbm, skip),
                (w_hbm, weight),
            ]
        )
    ]
    for load in loads:
        load.start()
    pending = []

    def at(zz, yy):
        return zz * ys + yy

    def signal(sem, s, c):
        pl.semaphore_signal(sem, inc=1, device_id=(s, c), device_id_type=MESH)

    right = lax.rem(x + 1, CHIPS) * CORES + core
    left = lax.rem(x + CHIPS - 1, CHIPS) * CORES + core
    sibling = x * CORES + 1 - core
    z_up = lax.rem(z + 1, zs)
    z_down = lax.rem(z + zs - 1, zs)

    barrier = pltpu.get_barrier_semaphore()
    for e in range(1, ys):
        signal(barrier, at(z, lax.rem(y + e, ys)), chan)
    for c in (right, left, sibling):
        signal(barrier, seq, c)
    for d in range(1, zs):

        @pl.when(z + d < zs)
        def _():
            signal(barrier, at(lax.rem(z + d, zs), y), chan)

    @pl.when(last_y & (z < zs - 1))
    def _():
        for e in range(ys):
            signal(barrier, at(z_up, e), chan)

    loads[0].wait()
    loads[1].wait()
    r = rate[...]
    series = r * (1.0 - r * (1 / 2) * (1.0 - r * (1 / 3) * (1.0 - r * (1 / 4) * (1.0 - r * (1 / 5) * (1.0 - r * (1 / 6))))))
    gain = res[...] * series
    decay = jnp.exp(-r)
    for m in range(MODES):
        rate3[m] = jnp.broadcast_to(r[m : m + 1], (SUBS, width))
        decay3[m] = jnp.broadcast_to(decay[m : m + 1], (SUBS, width))
        gain3[m] = jnp.broadcast_to(gain[m : m + 1], (SUBS, width))

    row = lax.broadcasted_iota(jnp.int32, (ROWS, ROWS), 0)
    col = lax.broadcasted_iota(jnp.int32, (ROWS, ROWS), 1)
    order = jnp.where(col == (row & 7) * STEPS + (row >> 3), 1.0, 0.0).astype(BF16)
    back = jnp.where(row == (col & 7) * STEPS + (col >> 3), 1.0, 0.0).astype(BF16)

    def arranged(block):
        return jnp.dot(order, block, preferred_element_type=F32).reshape(STEPS, SUBS, width)

    sub = lax.broadcasted_iota(jnp.int32, (SUBS, LANES), 0)
    sub3 = lax.broadcasted_iota(jnp.int32, (MODES, SUBS, LANES), 1)
    first = sub == 0
    subf3 = sub3.astype(F32)

    loads[2].wait()
    loads[3].wait()
    loads[4].wait()
    xk[...] = arranged(k_in[...])
    xv[...] = arranged(v_in[...])

    def lags(block):
        last = jnp.where(first, 0.0, pltpu.roll(block[STEPS - 1], 1, 0))
        last_but_one = jnp.where(first, 0.0, pltpu.roll(block[STEPS - 2], 1, 0))
        return lagged(block, last, last_but_one)

    for l in range(tiles):
        cols = slice(l * LANES, (l + 1) * LANES)
        kb, vb = xk[:, :, cols], xv[:, :, cols]
        g = tapped(taps, 1, cols, kb, *lags(kb)) * tapped(taps, 2, cols, vb, *lags(vb))
        g = jnp.concatenate([jnp.where(first[None], 0.0, g[:2]), g[2:]], axis=0)
        local[:, :, cols] = g
        a = decay3[:, :, cols]
        state = jnp.broadcast_to(g[0][None], a.shape)
        for j in range(1, STEPS):
            state = state * a + g[j][None]
        step = a
        for _ in range(4):
            step = step * step
        for reach in (1, 2, 4):
            state = state + jnp.where(sub3 >= reach, step, 0.0) * pltpu.roll(state, reach, 1)
            step = step * step
        enter[:, :, cols] = jnp.where(sub3 >= 1, pltpu.roll(state, 1, 1), 0.0)
        for m in range(MODES):
            state_y[y, m : m + 1, cols] = state[m, SUBS - 1 : SUBS, :]

    loads[5].wait()
    pick = lax.broadcasted_iota(jnp.int32, (MODES, ROWS), 0)
    pos = lax.broadcasted_iota(jnp.int32, (MODES, ROWS), 1)

    def chosen(base, block):
        i = pick - base
        ends = ((i >= 0) & (i < 2) & (pos == i)) | ((i >= 2) & (i < 4) & (pos == i + ROWS - 4))
        return jnp.dot(
            jnp.where(ends, 1.0, 0.0).astype(BF16), block[...], preferred_element_type=F32
        )

    edge_y[y] = (chosen(0, k_in) + chosen(4, v_in) + chosen(8, q_in)).astype(BF16)

    pl.semaphore_wait(barrier, (ys - 1) + 3 + z + jnp.where(z > 0, 1, 0))
    for d in range(1, zs):

        @pl.when(z >= d)
        def _():
            signal(ready.at[d - 1], at(lax.rem(z + zs - d, zs), y), chan)

    @pl.when(z > 0)
    def _():
        signal(ready_edge, at(z_down, ys - 1), chan)

    y_copies = []
    for e in range(1, ys):
        to = (at(z, lax.rem(y + e, ys)), chan)
        for i, buf in enumerate((state_y, edge_y)):
            copy = pltpu.make_async_remote_copy(
                buf.at[y], buf.at[y], y_send.at[i, e - 1], y_recv.at[i, e - 1],
                device_id=to, device_id_type=MESH,
            )
            copy.start()
            pending.append(copy.wait_send)
            y_copies.append(copy)

    edges = [
        pltpu.make_async_remote_copy(
            edge_y.at[y], edge_z, e_send.at[e], e_recv,
            device_id=(at(z_up, e), chan), device_id_type=MESH,
        )
        for e in range(ys)
    ]

    @pl.when(last_y & (z < zs - 1))
    def _():
        pl.semaphore_wait(ready_edge, ys)
        for copy in edges:
            copy.start()

    @pending.append
    def _():
        @pl.when(last_y & (z < zs - 1))
        def _():
            for copy in edges:
                copy.wait_send()

    loads[6].wait()
    for l in range(tiles):
        cols = slice(l * LANES, (l + 1) * LANES)
        r3, a, w = rate3[:, :, cols], decay3[:, :, cols], gain3[:, :, cols]
        wa = w * a
        enter[:, :, cols] = wa * enter[:, :, cols]
        power[:, :, cols] = wa * jnp.exp(-float(STEPS) * subf3 * r3)
        close = w * jnp.exp(-subf3 * r3)
        a8 = a * a
        a8 = a8 * a8
        a8 = a8 * a8
        near[0:SUBS, cols] = tree_sum(close)
        near[SUBS : 2 * SUBS, cols] = tree_sum(close * a8)
        g = local[:, :, cols]
        out = g * skip[0:1, cols]
        for d in range(STEPS):
            add = g[: STEPS - d] * near[d : d + 1, cols][None]
            out = out + add if d == 0 else jnp.concatenate([out[:d], out[d:] + add], axis=0)
        local[:, :, cols] = out
    for i in range(2):
        half_cols = slice(i * width // 2, (i + 1) * width // 2)
        arranged_q = jnp.dot(order, q_in[:, half_cols], preferred_element_type=F32)
        arranged_q = arranged_q.reshape(STEPS, SUBS, width // 2)
        for l in range(tiles // 2):
            cols = slice(i * width // 2 + l * LANES, i * width // 2 + (l + 1) * LANES)
            qb = arranged_q[:, :, l * LANES : (l + 1) * LANES]
            query[:, :, cols] = tapped(taps, 0, cols, qb, *lags(qb))
    r = rate[...]
    a126 = jnp.exp(-(ROWS - 2.0) * r)
    a127 = jnp.exp(-(ROWS - 1.0) * r)
    a128 = jnp.exp(-float(ROWS) * r)

    everything = slice(0, width)

    @pl.when(z == 0)
    def _():
        edge_z[...] = jnp.zeros_like(edge_z)

    @pl.when(z > 0)
    def _():
        edges[0].wait_recv()

    for copy in y_copies:
        copy.wait_recv()
    ends = edge_z[...].astype(F32)
    start = jnp.zeros_like(r)
    for e in range(ys):
        now = edge_y[e].astype(F32)
        k0, k1, v0, v1 = (now[i : i + 1] for i in (0, 1, 4, 5))
        k126, k127, v126, v127, q126, q127 = (ends[i : i + 1] for i in (2, 3, 6, 7, 10, 11))
        g0 = tapped(taps, 1, everything, k0, k127, k126) * tapped(
            taps, 2, everything, v0, v127, v126
        )
        g1 = tapped(taps, 1, everything, k1, k0, k127) * tapped(taps, 2, everything, v1, v0, v127)
        for i, line in enumerate((g0, g1, q126, q127)):
            heads[e, i : i + 1, :] = line
        starts[e] = start
        start = start * a128 + (state_y[e] + a127 * g0 + a126 * g1)
        ends = now
    total[...] = start

    z_copies = []
    for d in range(1, zs):
        copy = pltpu.make_async_remote_copy(
            total, ring_z.at[d - 1], z_send.at[d - 1], z_recv.at[d - 1],
            device_id=(at(lax.rem(z + d, zs), y), chan), device_id_type=MESH,
        )
        z_copies.append(copy)

        @pl.when(z + d < zs)
        def _():
            pl.semaphore_wait(ready.at[d - 1], 1)
            copy.start()

        pending.append(functools.partial(pl.when(z + d < zs), copy.wait_send))

    g0, g1, q126, q127 = (heads[y, i : i + 1, :] for i in range(4))
    for j in range(STEPS):
        extra = near[j : j + 1, :] * g0
        if j:
            extra = extra + near[j - 1 : j, :] * g1
        if j < 2:
            extra = extra + skip[0:1, :] * (g0, g1)[j]
        local[j, 0:1, :] += extra
    query[0, 0:1, :] += taps[0, 1:2, :] * q127 + taps[0, 2:3, :] * q126
    query[1, 0:1, :] += taps[0, 2:3, :] * q127
    head = jnp.exp(r) * g0 + jnp.exp(2.0 * r) * g1

    before[...] = jnp.zeros_like(before)
    for d in range(1, zs):

        @pl.when(z >= d)
        def _():
            z_copies[d - 1].wait_recv()
            before[...] += jnp.exp(-float(ROWS * ys * (d - 1)) * rate[...]) * ring_z[d - 1]

    start = starts[y] + jnp.exp(-float(ROWS) * y.astype(F32) * r) * before[...]
    hit[...] = start
    hit_later[...] = start + head

    def send(index, slot, piece, to_slot, to):
        copy = pltpu.make_async_remote_copy(
            hid.at[slot, piece], hid.at[to_slot, piece], g_send.at[index], g_recv.at[index],
            device_id=(seq, to), device_id_type=MESH,
        )
        copy.start()
        pending.append(copy.wait_send)
        return copy

    per = tiles // PIECES
    own_sib, own_right, own_left = {}, {}, {}
    for p in range(PIECES):
        for i in range(per):
            l = p * per + i
            cols = slice(l * LANES, (l + 1) * LANES)
            a = decay3[:, :, cols]
            state = jnp.stack(
                [
                    enter[m, :, cols]
                    + power[m, :, cols]
                    * jnp.where(first, hit[m : m + 1, cols], hit_later[m : m + 1, cols])
                    for m in range(MODES)
                ]
            )
            blocks = []
            for j in range(STEPS):
                blocks.append(query[j, :, cols] * (local[j, :, cols] + tree_sum(state)))
                if j < STEPS - 1:
                    state = state * a
            block = jnp.concatenate(blocks, axis=0)
            hid[0, p, :, i * LANES : (i + 1) * LANES] = block.astype(BF16)
        own_right[p] = send(p, 0, p, 6, right)
        own_sib[p] = send(2 + p, 0, p, 1, sibling)
    for p in (1, 0):
        own_left[p] = send(4 + p, 0, p, 2, left)

    loads[7].wait()
    half = width // PIECES

    def product(slot, piece):
        owner = lax.rem(x + slot // CORES, CHIPS) * CORES + (core if slot % CORES == 0 else 1 - core)
        rows = pl.ds(pl.multiple_of(owner * width + piece * half, half), half)
        return jnp.dot(hid[slot, piece], weight[rows, :], preferred_element_type=F32)

    acc[...] = product(0, 0) + product(0, 1)
    for p in range(PIECES):
        own_sib[p].wait_recv()
        acc[...] += product(1, p)

    own_right[0].wait_recv()
    on_right = send(6, 6, 0, 4, right)
    sib = {(7, 0): send(8, 6, 0, 7, sibling)}
    own_left[1].wait_recv()
    on_left = send(7, 2, 1, 4, left)
    sib[3, 1] = send(9, 2, 1, 3, sibling)
    acc[...] += product(6, 0) + product(2, 1)
    for slot, p in ((7, 0), (3, 1)):
        sib[slot, p].wait_recv()
        acc[...] += product(slot, p)
    own_right[1].wait_recv()
    sib[7, 1] = send(10, 6, 1, 7, sibling)
    own_left[0].wait_recv()
    sib[3, 0] = send(11, 2, 0, 3, sibling)
    acc[...] += product(6, 1) + product(2, 0)
    for slot, p in ((7, 1), (3, 0)):
        sib[slot, p].wait_recv()
        acc[...] += product(slot, p)
    on_right.wait_recv()
    sib[5, 0] = send(12, 4, 0, 5, sibling)
    on_left.wait_recv()
    sib[5, 1] = send(13, 4, 1, 5, sibling)
    acc[...] += product(4, 0) + product(4, 1)
    for p in range(PIECES):
        sib[5, p].wait_recv()
        acc[...] += product(5, p)

    mixed = acc[...].astype(BF16)
    out_ref[...] = jnp.dot(back, mixed, preferred_element_type=F32).astype(BF16)

    for wait in pending:
        wait()


def per_device(zs, ys, query, key, value, short_taps, residue, rate, skip, out_weight):
    width = query.shape[1]
    modes = pltpu.VMEM((MODES, width), F32)
    table = pltpu.VMEM((MODES, SUBS, width), F32)
    block = pltpu.VMEM((STEPS, SUBS, width), F32)
    dma = pltpu.SemaphoreType.DMA
    regular = pltpu.SemaphoreType.REGULAR
    scratch = [
        pltpu.VMEM((ROWS, width), BF16),
        pltpu.VMEM((ROWS, width), BF16),
        pltpu.VMEM((ROWS, width), BF16),
        pltpu.VMEM(short_taps.shape, F32),
        modes,
        modes,
        pltpu.VMEM((1, width), F32),
        pltpu.VMEM(out_weight.shape, BF16),
        table,
        table,
        table,
        block,
        block,
        table,
        table,
        pltpu.VMEM((STEPS, width), F32),
        block,
        block,
        pltpu.VMEM((ys, MODES, width), BF16),
        pltpu.VMEM((MODES, width), BF16),
        pltpu.VMEM((ys, MODES, width), F32),
        pltpu.VMEM((ys, 8, width), F32),
        pltpu.VMEM((ys, MODES, width), F32),
        modes,
        pltpu.VMEM((zs - 1, MODES, width), F32),
        modes,
        modes,
        modes,
        pltpu.VMEM((CHIPS * CORES, PIECES, ROWS, width // PIECES), BF16),
        pltpu.VMEM((ROWS, width), F32),
        dma((8,)),
        dma((2, ys - 1)),
        dma((2, ys - 1)),
        dma((ys,)),
        dma,
        dma((zs - 1,)),
        dma((zs - 1,)),
        dma((14,)),
        dma((14,)),
        regular((zs - 1,)),
        regular,
    ]
    return pl.pallas_call(
        functools.partial(kernel, zs, ys),
        out_shape=jax.ShapeDtypeStruct((ROWS, width), BF16),
        in_specs=[pl.BlockSpec(memory_space=pl.ANY)] * 8,
        out_specs=pl.BlockSpec(memory_space=pltpu.VMEM),
        scratch_shapes=scratch,
        compiler_params=pltpu.CompilerParams(
            collective_id=0, has_side_effects=True, vmem_limit_bytes=56 * 1024 * 1024
        ),
    )(query, key, value, short_taps, residue.T, rate.T, skip[None, :], out_weight)


def solution(mesh, ys=4):
    placed = (
        P("seq", "chan"),
        P("seq", "chan"),
        P("seq", "chan"),
        P(None, None, "chan"),
        P("chan", None),
        P("chan", None),
        P("chan"),
        P(None, "chan"),
    )
    return jax.shard_map(
        functools.partial(per_device, mesh.shape["seq"] // ys, ys),
        mesh=mesh,
        in_specs=placed,
        out_specs=P("seq", "chan"),
        check_vma=False,
    )
```

time: 30.3 us -> 30.1 us (level)
  the two profiles are of different devices: /device:TPU:33 before, /device:TPU:225 now
where the time goes in v2:
time: 30.1 us; the launch traced here: 30 us
  Pallas kernels  28.4 us (94%)
  local copies, waits for them, and re-layouts  1.57 us (5%)
    pallas_call x1, Pallas kernels, per_device(): pl.pallas_call(functools.partial(kernel, zs, ys), out_shape=jax.ShapeDtyp...  28.4 us
    unnamed x1, local copies, waits for them, and re-layouts  1.57 us

profile of v2, /device:TPU:225, one launch (start us, length us, event | category | flops | bytes accessed | tf_op | source)
XLA Modules:
  0.0 30.0 jit_solution(15078327690215285728)
XLA Ops:
  0.0 28.4 %shard_map.82 = bf16[128,512]{1,0:T(8,128)(2,1)} custom-call(bf16[128,512]{1,0:T(8,128)(2,1)} %q_hbm.1, bf16[128,512]{1,0:T(8,128)(2,1)} %k_hbm.1, bf16[128,512]{1,0:T(8,128)(2,1)} %v_hbm.1, f32[3,3,512]{2,1,0:T(4,128)} %taps_hbm.1, f32[16,512]{1,0:T(8,128)} %bitcast.3, f32[16,512]{1,0:T(8,128)} %bitcast.4, f32[1,512]{1,0:T(1,128)} %bitcast.5, ...), custom_call_target="tpu_custom_call" | custom-call | tf_op jit(solution)/shard_map/pallas_call | solution.py:496
  28.4 1.6 %copy.10 = bf16[128,512]{1,0:T(8,128)(2,1)} copy(bf16[128,512]{1,0:T(8,128)(2,1)} %shard_map.82) | data formatting | bytes 262144

commit v3 on v2

v3 whole, which is shorter than its diff:
```python
import functools

import jax
import jax.numpy as jnp
import ml_dtypes
import numpy as np
from jax import lax
from jax.experimental import pallas as pl
from jax.experimental.pallas import tpu as pltpu
from jax.sharding import PartitionSpec as P

MESH = pl.DeviceIdType.MESH
F32 = jnp.float32
BF16 = jnp.bfloat16
MODES = 16
STEPS = 16
SUBS = 8
ROWS = STEPS * SUBS
LANES = 128
CHIPS = 4
CORES = 2
PIECES = 2
NODES = STEPS - 2


def tree_sum(array):
    while array.shape[0] > 1:
        half = array.shape[0] // 2
        array = array[:half] + array[half:]
    return array[0]


def lagged(block, last, last_but_one):
    one = jnp.concatenate([last[None], block[:-1]], axis=0)
    two = jnp.concatenate([last_but_one[None], one[:-1]], axis=0)
    return one, two


def tapped(taps, which, cols, now, one, two):
    return (
        taps[which, 0:1, cols] * now + taps[which, 1:2, cols] * one + taps[which, 2:3, cols] * two
    )


def kernel(
    zs,
    ys,
    q_hbm,
    k_hbm,
    v_hbm,
    taps_hbm,
    res_hbm,
    rate_hbm,
    skip_hbm,
    w_hbm,
    weights_hbm,
    places_hbm,
    out_ref,
    q_in,
    k_in,
    v_in,
    taps,
    res,
    rate,
    skip,
    weight,
    weights,
    places,
    rate3,
    decay3,
    gain3,
    xq,
    xk,
    xv,
    enter,
    local,
    near,
    node3,
    msg,
    ring_y,
    edge_z,
    total,
    ring_z,
    before,
    flow_out,
    flow,
    hid,
    acc,
    load_sem,
    y_send,
    y_recv,
    e_send,
    e_recv,
    z_send,
    z_recv,
    g_send,
    g_recv,
    f_send,
    f_recv,
    ready_x,
    ready_y,
    ready_z,
    ready_edge,
):
    seq = lax.axis_index("seq")
    chan = lax.axis_index("chan")
    z, y = seq // ys, lax.rem(seq, ys)
    x, core = chan // CORES, lax.rem(chan, CORES)
    width = k_in.shape[1]
    tiles = width // LANES
    half = width // PIECES
    per = tiles // PIECES
    last_y = y == ys - 1

    loads = [
        pltpu.make_async_copy(src, dst, load_sem.at[i])
        for i, (src, dst) in enumerate(
            [
                (rate_hbm, rate),
                (res_hbm, res),
                (taps_hbm, taps),
                (k_hbm, k_in),
                (v_hbm, v_in),
                (q_hbm, q_in),
                (skip_hbm, skip),
                (places_hbm, places),
                (weights_hbm, weights),
                (w_hbm, weight),
            ]
        )
    ]
    for load in loads:
        load.start()
    pending = []

    def at(zz, yy):
        return zz * ys + yy

    def signal(sem, s, c):
        pl.semaphore_signal(sem, inc=1, device_id=(s, c), device_id_type=MESH)

    def wait_for(sem, amount):
        pl.when(amount > 0)(lambda: pl.semaphore_wait(sem, amount))

    def x_peer(e):
        return lax.rem(x + e, CHIPS) * CORES

    right = x_peer(1) + core
    left = x_peer(CHIPS - 1) + core
    sibling = x * CORES + 1 - core
    z_up = lax.rem(z + 1, zs)
    z_down = lax.rem(z + zs - 1, zs)

    barrier = pltpu.get_barrier_semaphore()
    for e in range(1, CHIPS):

        @pl.when(x + e < CHIPS)
        def _():
            for c in range(CORES):
                signal(barrier, seq, x_peer(e) + c)

    @pl.when(core == 1)
    def _():
        signal(barrier, seq, sibling)

    for e in range(1, ys):

        @pl.when(y + e < ys)
        def _():
            signal(barrier, at(z, lax.rem(y + e, ys)), chan)

    for d in range(1, zs):

        @pl.when(z + d < zs)
        def _():
            signal(barrier, at(lax.rem(z + d, zs), y), chan)

    @pl.when(last_y & (z < zs - 1))
    def _():
        for e in range(ys):
            signal(barrier, at(z_up, e), chan)

    wait_for(barrier, CORES * x + (1 - core) + y + z + jnp.where(z > 0, 1, 0))
    for d in range(1, zs):

        @pl.when(z >= d)
        def _():
            signal(ready_z.at[d - 1], at(lax.rem(z + zs - d, zs), y), chan)

    for e in range(1, ys):

        @pl.when(y >= e)
        def _():
            signal(ready_y, at(z, lax.rem(y + ys - e, ys)), chan)

    for e in range(1, CHIPS):

        @pl.when(x >= e)
        def _():
            for c in range(CORES):
                signal(ready_x, seq, x_peer(CHIPS - e) + c)

    @pl.when(core == 0)
    def _():
        signal(ready_x, seq, sibling)

    @pl.when(z > 0)
    def _():
        signal(ready_edge, at(z_down, ys - 1), chan)

    loads[0].wait()
    loads[1].wait()
    r = rate[...]
    series = r * (1.0 - r * (1 / 2) * (1.0 - r * (1 / 3) * (1.0 - r * (1 / 4) * (1.0 - r * (1 / 5) * (1.0 - r * (1 / 6))))))
    gain = res[...] * series
    decay = jnp.exp(-r)
    for m in range(MODES):
        rate3[m] = jnp.broadcast_to(r[m : m + 1], (SUBS, width))
        decay3[m] = jnp.broadcast_to(decay[m : m + 1], (SUBS, width))
        gain3[m] = jnp.broadcast_to(gain[m : m + 1], (SUBS, width))

    row = lax.broadcasted_iota(jnp.int32, (ROWS, ROWS), 0)
    col = lax.broadcasted_iota(jnp.int32, (ROWS, ROWS), 1)
    order = jnp.where(col == (row & 7) * STEPS + (row >> 3), 1.0, 0.0).astype(BF16)
    back = jnp.where(row == (col & 7) * STEPS + (col >> 3), 1.0, 0.0).astype(BF16)

    def arranged(block):
        return jnp.dot(order, block, preferred_element_type=F32).reshape(STEPS, SUBS, width)

    sub = lax.broadcasted_iota(jnp.int32, (SUBS, LANES), 0)
    sub3 = lax.broadcasted_iota(jnp.int32, (MODES, SUBS, LANES), 1)
    first = sub == 0
    subf3 = sub3.astype(F32)

    for i in (2, 3, 4, 5):
        loads[i].wait()
    xk[...] = arranged(k_in[...])
    xv[...] = arranged(v_in[...])
    xq[...] = arranged(q_in[...])

    def lags(block):
        last = jnp.where(first, 0.0, pltpu.roll(block[STEPS - 1], 1, 0))
        last_but_one = jnp.where(first, 0.0, pltpu.roll(block[STEPS - 2], 1, 0))
        return lagged(block, last, last_but_one)

    for l in range(tiles):
        cols = slice(l * LANES, (l + 1) * LANES)
        kb, vb = xk[:, :, cols], xv[:, :, cols]
        g = tapped(taps, 1, cols, kb, *lags(kb)) * tapped(taps, 2, cols, vb, *lags(vb))
        g = jnp.concatenate([jnp.where(first[None], 0.0, g[:2]), g[2:]], axis=0)
        local[:, :, cols] = g
        a = decay3[:, :, cols]
        state = jnp.broadcast_to(g[0][None], a.shape)
        for j in range(1, STEPS):
            state = state * a + g[j][None]
        step = a
        for _ in range(4):
            step = step * step
        for reach in (1, 2, 4):
            state = state + jnp.where(sub3 >= reach, step, 0.0) * pltpu.roll(state, reach, 1)
            step = step * step
        enter[:, :, cols] = jnp.where(sub3 >= 1, pltpu.roll(state, 1, 1), 0.0)
        for m in range(MODES):
            msg[l, m : m + 1, :] = state[m, SUBS - 1 : SUBS, :]
        for i, block in enumerate((xk, xv, xq)):
            for n, (j, s) in enumerate(((0, 0), (1, 0), (STEPS - 2, SUBS - 1), (STEPS - 1, SUBS - 1))):
                line = MODES + 4 * i + n
                msg[l, line : line + 1, :] = block[j, s : s + 1, cols]
        msg[l, MODES + 12 : MODES + 16, :] = jnp.zeros((4, LANES), F32)

    wait_for(ready_x, CORES * (CHIPS - 1 - x) + core)
    wait_for(ready_y, ys - 1 - y)
    y_copies = []
    for e in range(1, ys):
        to = lax.rem(y + e, ys)
        copy = pltpu.make_async_remote_copy(
            msg.at[to], ring_y.at[y], y_send.at[e - 1], y_recv.at[e - 1],
            device_id=(at(z, to), chan), device_id_type=MESH,
        )
        copy.start()
        pending.append(copy.wait_send)
        y_copies.append(copy)
    ring_y[y] = msg[y]

    def send(index, slot, piece, to_slot, to):
        copy = pltpu.make_async_remote_copy(
            hid.at[slot, piece], hid.at[to_slot, piece], g_send.at[index], g_recv.at[index],
            device_id=(seq, to), device_id_type=MESH,
        )
        copy.start()
        pending.append(copy.wait_send)
        return copy

    loads[6].wait()
    own_sib, own_right, own_left = {}, {}, {}
    for p in range(PIECES):
        for i in range(per):
            l = p * per + i
            cols = slice(l * LANES, (l + 1) * LANES)
            r3, a, w = rate3[:, :, cols], decay3[:, :, cols], gain3[:, :, cols]
            close = w * jnp.exp(-subf3 * r3)
            a8 = a * a
            a8 = a8 * a8
            a8 = a8 * a8
            near[0:SUBS, cols] = tree_sum(close)
            near[SUBS : 2 * SUBS, cols] = tree_sum(close * a8)
            g = local[:, :, cols]
            out = g * skip[0:1, cols]
            for d in range(STEPS):
                add = g[: STEPS - d] * near[d : d + 1, cols][None]
                out = out + add if d == 0 else jnp.concatenate([out[:d], out[d:] + add], axis=0)
            qb = xq[:, :, cols]
            qb = tapped(taps, 0, cols, qb, *lags(qb))
            state = w * a * enter[:, :, cols]
            own, factor = [], []
            for j in range(STEPS):
                line = qb[j] * (out[j] + tree_sum(state))
                if j < STEPS - 1:
                    state = state * a
                own.append(jnp.where(first, 0.0, line) if j < 2 else line)
                factor.append(jnp.where(first, 1.0, qb[j]) if j < 2 else qb[j])
            to = slice(i * LANES, (i + 1) * LANES)
            hid[0, p, 0, :, to] = jnp.concatenate(own, axis=0).astype(BF16)
            hid[0, p, 1, :, to] = jnp.concatenate(factor, axis=0).astype(BF16)
        own_right[p] = send(p, 0, p, 6, right)
        own_sib[p] = send(2 + p, 0, p, 1, sibling)
    for p in (1, 0):
        own_left[p] = send(4 + p, 0, p, 2, left)

    edges = [
        pltpu.make_async_remote_copy(
            msg.at[e, pl.ds(MODES, 16)], edge_z, e_send.at[e], e_recv,
            device_id=(at(z_up, e), chan), device_id_type=MESH,
        )
        for e in range(ys)
    ]

    @pl.when(last_y & (z < zs - 1))
    def _():
        pl.semaphore_wait(ready_edge, ys)
        for copy in edges:
            copy.start()

    @pending.append
    def _():
        @pl.when(last_y & (z < zs - 1))
        def _():
            for copy in edges:
                copy.wait_send()

    mine = pl.ds(pl.multiple_of(y * LANES, LANES), LANES)
    r = rate[:, mine]
    a126 = jnp.exp(-(ROWS - 2.0) * r)
    a127 = jnp.exp(-(ROWS - 1.0) * r)
    a128 = jnp.exp(-float(ROWS) * r)
    loads[7].wait()
    for m in range(MODES):
        node3[m] = gain3[m, 0:1, mine] * jnp.exp(-(places[...] + 1.0) * rate[m : m + 1, mine])

    @pl.when(z == 0)
    def _():
        edge_z[...] = jnp.zeros_like(edge_z)

    @pl.when(z > 0)
    def _():
        edges[0].wait_recv()

    for copy in y_copies:
        copy.wait_recv()
    ends = edge_z[...]
    start = jnp.zeros_like(r)
    starts, heads = [], []
    for e in range(ys):
        now = ring_y[e, MODES : MODES + 16, :]
        k0, k1, v0, v1, q0, q1 = (now[i : i + 1] for i in (0, 1, 4, 5, 8, 9))
        k126, k127, v126, v127, q126, q127 = (ends[i : i + 1] for i in (2, 3, 6, 7, 10, 11))
        g0 = tapped(taps, 1, mine, k0, k127, k126) * tapped(taps, 2, mine, v0, v127, v126)
        g1 = tapped(taps, 1, mine, k1, k0, k127) * tapped(taps, 2, mine, v1, v0, v127)
        s0 = tapped(taps, 0, mine, q0, q127, q126)
        s1 = tapped(taps, 0, mine, q1, q0, q127)
        heads.append((g0, g1, s0, s1))
        starts.append(start)
        start = start * a128 + (ring_y[e, 0:MODES, :] + a127 * g0 + a126 * g1)
        ends = now
    total[...] = start

    z_copies = []
    for d in range(1, zs):
        copy = pltpu.make_async_remote_copy(
            total, ring_z.at[d - 1], z_send.at[d - 1], z_recv.at[d - 1],
            device_id=(at(lax.rem(z + d, zs), y), chan), device_id_type=MESH,
        )
        z_copies.append(copy)

        @pl.when(z + d < zs)
        def _():
            pl.semaphore_wait(ready_z.at[d - 1], 1)
            copy.start()

        pending.append(functools.partial(pl.when(z + d < zs), copy.wait_send))

    own_right[0].wait_recv()
    on_right = send(6, 6, 0, 4, right)
    own_left[1].wait_recv()
    on_left = send(7, 2, 1, 4, left)
    sib = {(7, 0): send(8, 6, 0, 7, sibling), (3, 1): send(11, 2, 1, 3, sibling)}

    before[...] = jnp.zeros_like(before)
    for d in range(1, zs):

        @pl.when(z >= d)
        def _():
            z_copies[d - 1].wait_recv()
            before[...] += jnp.exp(-float(ROWS * ys * (d - 1)) * rate[:, mine]) * ring_z[d - 1]

    sums = before[...]
    rows = lax.broadcasted_iota(jnp.int32, (STEPS, LANES), 0)
    near0, near1, direct = near[0:1, mine], near[1:2, mine], skip[0:1, mine]
    up1, up2 = jnp.exp(r), jnp.exp(2.0 * r)
    for e in range(ys):
        g0, g1, s0, s1 = heads[e]
        entering = sums + starts[e]
        later = entering + up1 * g0 + up2 * g1
        values = jnp.zeros((STEPS, LANES), F32)
        for m in range(MODES):
            values += node3[m] * jnp.where(rows < NODES, later[m : m + 1], entering[m : m + 1])
        h0 = s0 * (values[NODES : NODES + 1] + (near0 + direct) * g0)
        h1 = s1 * (values[NODES + 1 : NODES + 2] + near1 * g0 + (near0 + direct) * g1)
        values = jnp.where(rows == NODES, h0, jnp.where(rows == NODES + 1, h1, values))
        flow_out[e] = values.astype(BF16)
        sums = sums * a128

    f_copies = {}
    for ey in range(ys):
        to_y = lax.rem(y + ey, ys)
        for ex in range(CHIPS):
            for ec in range(CORES):
                if ex == ec == ey == 0:
                    continue
                slot = ex * CORES + ec
                to_c = x_peer(CHIPS - ex) + (core if ec == 0 else 1 - core)
                copy = pltpu.make_async_remote_copy(
                    flow_out.at[to_y], flow.at[slot, y], f_send.at[slot, ey], f_recv.at[slot, ey],
                    device_id=(at(z, to_y), to_c), device_id_type=MESH,
                )
                copy.start()
                pending.append(copy.wait_send)
                f_copies[slot, ey] = copy
    flow[0, y] = flow_out[y]

    own_right[1].wait_recv()
    sib[7, 1] = send(9, 6, 1, 7, sibling)
    own_left[0].wait_recv()
    sib[3, 0] = send(10, 2, 0, 3, sibling)
    on_right.wait_recv()
    sib[5, 0] = send(12, 4, 0, 5, sibling)
    on_left.wait_recv()
    sib[5, 1] = send(13, 4, 1, 5, sibling)

    loads[8].wait()
    loads[9].wait()
    for n, slot in enumerate((0, 1, 6, 2, 7, 3, 4, 5)):
        for p in range(PIECES):
            if slot == 1:
                own_sib[p].wait_recv()
            if slot in (3, 5, 7):
                sib[slot, p].wait_recv()
        for ey in range(ys):
            if slot or ey:
                f_copies[slot, ey].wait_recv()
        values = jnp.concatenate([flow[slot, l] for l in range(tiles)], axis=1)
        entering = jnp.dot(
            weights[...], jnp.concatenate([values, values], axis=0), preferred_element_type=F32
        )
        blocks = []
        for p in range(PIECES):
            own, factor = hid[slot, p, 0].astype(F32), hid[slot, p, 1].astype(F32)
            blocks.append((own + factor * entering[:, p * half : (p + 1) * half]).astype(BF16))
        owner = x_peer(slot // CORES) + (core if slot % CORES == 0 else 1 - core)
        wrows = weight[pl.ds(pl.multiple_of(owner * width, width), width), :]
        part = jnp.dot(jnp.concatenate(blocks, axis=1), wrows, preferred_element_type=F32)
        if n:
            part = part + acc[...]
        acc[...] = part

    mixed = acc[...].astype(BF16)
    out_ref[...] = jnp.dot(back, mixed, preferred_element_type=F32).astype(BF16)

    for wait in pending:
        wait()


def interpolation():
    turn = np.pi * (2 * np.arange(NODES) + 1) / (2 * NODES)
    places = ((ROWS - 1) / 2 * (1 - np.cos(turn))).astype(np.float32)
    at = places.astype(np.float64)
    share = np.array([1 / np.prod(at[i] - np.delete(at, i)) for i in range(NODES)])
    weights = np.zeros((ROWS, STEPS))
    for t in range(2, ROWS):
        part = share / (t - at)
        weights[t, :NODES] = part / part.sum()
    weights[0, NODES] = weights[1, NODES + 1] = 1
    weights = weights.reshape(SUBS, STEPS, STEPS).swapaxes(0, 1).reshape(ROWS, STEPS)
    high = weights.astype(ml_dtypes.bfloat16)
    low = (weights - high.astype(np.float64)).astype(ml_dtypes.bfloat16)
    places = np.broadcast_to(np.append(places, [0, 1]).astype(np.float32)[:, None], (STEPS, LANES))
    return np.concatenate([high, low], axis=1), np.ascontiguousarray(places)


def per_device(zs, ys, query, key, value, short_taps, residue, rate, skip, out_weight):
    width = query.shape[1]
    tiles = width // LANES
    weights, places = interpolation()
    modes = pltpu.VMEM((MODES, width), F32)
    tile = pltpu.VMEM((MODES, LANES), F32)
    table = pltpu.VMEM((MODES, SUBS, width), F32)
    block = pltpu.VMEM((STEPS, SUBS, width), F32)
    dma = pltpu.SemaphoreType.DMA
    regular = pltpu.SemaphoreType.REGULAR
    scratch = [
        pltpu.VMEM((ROWS, width), BF16),
        pltpu.VMEM((ROWS, width), BF16),
        pltpu.VMEM((ROWS, width), BF16),
        pltpu.VMEM(short_taps.shape, F32),
        modes,
        modes,
        pltpu.VMEM((1, width), F32),
        pltpu.VMEM(out_weight.shape, BF16),
        pltpu.VMEM(weights.shape, BF16),
        pltpu.VMEM(places.shape, F32),
        table,
        table,
        table,
        block,
        block,
        block,
        table,
        block,
        pltpu.VMEM((STEPS, width), F32),
        pltpu.VMEM((MODES, STEPS, LANES), F32),
        pltpu.VMEM((tiles, MODES + 16, LANES), F32),
        pltpu.VMEM((ys, MODES + 16, LANES), F32),
        pltpu.VMEM((16, LANES), F32),
        tile,
        pltpu.VMEM((zs - 1, MODES, LANES), F32),
        tile,
        pltpu.VMEM((ys, STEPS, LANES), BF16),
        pltpu.VMEM((CHIPS * CORES, tiles, STEPS, LANES), BF16),
        pltpu.VMEM((CHIPS * CORES, PIECES, 2, ROWS, width // PIECES), BF16),
        pltpu.VMEM((ROWS, width), F32),
        dma((10,)),
        dma((ys - 1,)),
        dma((ys - 1,)),
        dma((ys,)),
        dma,
        dma((zs - 1,)),
        dma((zs - 1,)),
        dma((14,)),
        dma((14,)),
        dma((CHIPS * CORES, ys)),
        dma((CHIPS * CORES, ys)),
        regular,
        regular,
        regular((zs - 1,)),
        regular,
    ]
    return pl.pallas_call(
        functools.partial(kernel, zs, ys),
        out_shape=jax.ShapeDtypeStruct((ROWS, width), BF16),
        in_specs=[pl.BlockSpec(memory_space=pl.ANY)] * 10,
        out_specs=pl.BlockSpec(memory_space=pltpu.VMEM),
        scratch_shapes=scratch,
        compiler_params=pltpu.CompilerParams(
            collective_id=0, has_side_effects=True, vmem_limit_bytes=56 * 1024 * 1024
        ),
    )(
        query,
        key,
        value,
        short_taps,
        residue.T,
        rate.T,
        skip[None, :],
        out_weight,
        jnp.asarray(weights),
        jnp.asarray(places),
    )


def solution(mesh, ys=4):
    placed = (
        P("seq", "chan"),
        P("seq", "chan"),
        P("seq", "chan"),
        P(None, None, "chan"),
        P("chan", None),
        P("chan", None),
        P("chan"),
        P(None, "chan"),
    )
    return jax.shard_map(
        functools.partial(per_device, mesh.shape["seq"] // ys, ys),
        mesh=mesh,
        in_specs=placed,
        out_specs=P("seq", "chan"),
        check_vma=False,
    )
```

time: 30.1 us -> 25 us (0.83)
  Pallas kernels: 28.4 us -> 23.1 us
    pallas_call x1, Pallas kernels: 28.4 us -> 23.1 us  [per_device(): pl.pallas_call(functools.partial(kernel, zs, ys), out_shape=jax.ShapeDtyp...]
where the time goes in v3:
time: 25 us; the launch traced here: 24.6 us
  Pallas kernels  23.1 us (92%)
  local copies, waits for them, and re-layouts  1.57 us (6%)
    pallas_call x1, Pallas kernels, per_device(): pl.pallas_call(functools.partial(kernel, zs, ys), out_shape=jax.ShapeDtyp...  23.1 us
    unnamed x1, local copies, waits for them, and re-layouts  1.57 us

profile of v3, /device:TPU:225, one launch (start us, length us, event | category | flops | bytes accessed | tf_op | source)
XLA Modules:
  0.0 24.6 jit_solution(13231508605628262571)
XLA Ops:
  0.0 23.1 %shard_map.100 = bf16[128,512]{1,0:T(8,128)(2,1)} custom-call(bf16[128,512]{1,0:T(8,128)(2,1)} %q_hbm.1, bf16[128,512]{1,0:T(8,128)(2,1)} %k_hbm.1, bf16[128,512]{1,0:T(8,128)(2,1)} %v_hbm.1, f32[3,3,512]{2,1,0:T(4,128)} %taps_hbm.1, f32[16,512]{1,0:T(8,128)} %bitcast.3, f32[16,512]{1,0:T(8,128)} %bitcast.4, f32[1,512]{1,0:T(1,128)} %bitcast.5, ...), custom_call_target="tpu_custom_call" | custom-call | tf_op jit(solution)/shard_map/pallas_call | solution.py:567
  23.1 1.6 %copy.12 = bf16[128,512]{1,0:T(8,128)(2,1)} copy(bf16[128,512]{1,0:T(8,128)(2,1)} %shard_map.100) | data formatting | bytes 262144

commit v4 on v3

--- a/solution.py
+++ b/solution.py
@@ -20,6 +20,17 @@
 CHIPS = 4
 CORES = 2
 PIECES = 2
+FACTOR, OWN = 0, 1
+ROUTES = (
+    (0, 6, "right"),
+    (0, 2, "left"),
+    (0, 1, "sibling"),
+    (6, 4, "right"),
+    (2, 4, "left"),
+    (6, 7, "sibling"),
+    (2, 3, "sibling"),
+    (4, 5, "sibling"),
+)
 NODES = STEPS - 2
 
 
@@ -74,6 +85,7 @@
     xv,
     enter,
     local,
+    query,
     near,
     node3,
     msg,
@@ -151,6 +163,7 @@
     z_up = lax.rem(z + 1, zs)
     z_down = lax.rem(z + zs - 1, zs)
 
+    hub = zs // 2
     barrier = pltpu.get_barrier_semaphore()
     for e in range(1, CHIPS):
 
@@ -171,19 +184,31 @@
 
     for d in range(1, zs):
 
-        @pl.when(z + d < zs)
+        @pl.when((z + d < zs) & (z < hub))
         def _():
             signal(barrier, at(lax.rem(z + d, zs), y), chan)
 
-    @pl.when(last_y & (z < zs - 1))
+    @pl.when(last_y & (z < hub))
     def _():
         for e in range(ys):
             signal(barrier, at(z_up, e), chan)
 
-    wait_for(barrier, CORES * x + (1 - core) + y + z + jnp.where(z > 0, 1, 0))
+    @pl.when(z > hub)
+    def _():
+        signal(barrier, at(z_down, ys - 1), chan)
+
+    wait_for(
+        barrier,
+        CORES * x
+        + (1 - core)
+        + y
+        + jnp.minimum(z, hub)
+        + jnp.where((z > 0) & (z <= hub), 1, 0)
+        + jnp.where(last_y & (z >= hub) & (z < zs - 1), ys, 0),
+    )
     for d in range(1, zs):
 
-        @pl.when(z >= d)
+        @pl.when((z >= d) & (z - d < hub))
         def _():
             signal(ready_z.at[d - 1], at(lax.rem(z + zs - d, zs), y), chan)
 
@@ -204,7 +229,7 @@
     def _():
         signal(ready_x, seq, sibling)
 
-    @pl.when(z > 0)
+    @pl.when((z > 0) & (z <= hub))
     def _():
         signal(ready_edge, at(z_down, ys - 1), chan)
 
@@ -245,6 +270,12 @@
 
     for l in range(tiles):
         cols = slice(l * LANES, (l + 1) * LANES)
+        qb = xq[:, :, cols]
+        qb = tapped(taps, 0, cols, qb, *lags(qb))
+        query[:, :, cols] = qb
+        qb = jnp.concatenate([jnp.where(first[None], 1.0, qb[:2]), qb[2:]], axis=0)
+        to = slice(l % per * LANES, (l % per + 1) * LANES)
+        hid[0, FACTOR, l // per, :, to] = qb.reshape(ROWS, LANES).astype(BF16)
         kb, vb = xk[:, :, cols], xv[:, :, cols]
         g = tapped(taps, 1, cols, kb, *lags(kb)) * tapped(taps, 2, cols, vb, *lags(vb))
         g = jnp.concatenate([jnp.where(first[None], 0.0, g[:2]), g[2:]], axis=0)
@@ -282,17 +313,32 @@
         y_copies.append(copy)
     ring_y[y] = msg[y]
 
-    def send(index, slot, piece, to_slot, to):
+    g_copies = {}
+
+    def send(route, kind, piece):
+        slot, to_slot, to = ROUTES[route]
+        to = {"right": right, "left": left, "sibling": sibling}[to]
         copy = pltpu.make_async_remote_copy(
-            hid.at[slot, piece], hid.at[to_slot, piece], g_send.at[index], g_recv.at[index],
-            device_id=(seq, to), device_id_type=MESH,
+            hid.at[slot, kind, piece],
+            hid.at[to_slot, kind, piece],
+            g_send.at[route, kind, piece],
+            g_recv.at[route, kind, piece],
+            device_id=(seq, to),
+            device_id_type=MESH,
         )
         copy.start()
         pending.append(copy.wait_send)
-        return copy
+        g_copies[route, kind, piece] = copy
+
+    def arrived(route, kind, piece):
+        g_copies[route, kind, piece].wait_recv()
+
+    for kind in (FACTOR,):
+        for p in range(PIECES):
+            for route, piece in ((0, p), (1, PIECES - 1 - p), (2, p)):
+                send(route, kind, piece)
 
     loads[6].wait()
-    own_sib, own_right, own_left = {}, {}, {}
     for p in range(PIECES):
         for i in range(per):
             l = p * per + i
@@ -309,23 +355,19 @@
             for d in range(STEPS):
                 add = g[: STEPS - d] * near[d : d + 1, cols][None]
                 out = out + add if d == 0 else jnp.concatenate([out[:d], out[d:] + add], axis=0)
-            qb = xq[:, :, cols]
-            qb = tapped(taps, 0, cols, qb, *lags(qb))
             state = w * a * enter[:, :, cols]
-            own, factor = [], []
+            own = []
             for j in range(STEPS):
-                line = qb[j] * (out[j] + tree_sum(state))
+                line = query[j, :, cols] * (out[j] + tree_sum(state))
                 if j < STEPS - 1:
                     state = state * a
                 own.append(jnp.where(first, 0.0, line) if j < 2 else line)
-                factor.append(jnp.where(first, 1.0, qb[j]) if j < 2 else qb[j])
             to = slice(i * LANES, (i + 1) * LANES)
-            hid[0, p, 0, :, to] = jnp.concatenate(own, axis=0).astype(BF16)
-            hid[0, p, 1, :, to] = jnp.concatenate(factor, axis=0).astype(BF16)
-        own_right[p] = send(p, 0, p, 6, right)
-        own_sib[p] = send(2 + p, 0, p, 1, sibling)
-    for p in (1, 0):
-        own_left[p] = send(4 + p, 0, p, 2, left)
+            hid[0, OWN, p, :, to] = jnp.concatenate(own, axis=0).astype(BF16)
+        send(0, OWN, p)
+        send(2, OWN, p)
+    for p in reversed(range(PIECES)):
+        send(1, OWN, p)
 
     edges = [
         pltpu.make_async_remote_copy(
@@ -335,9 +377,12 @@
         for e in range(ys)
     ]
 
+    @pl.when(last_y & (z < hub))
+    def _():
+        pl.semaphore_wait(ready_edge, ys)
+
     @pl.when(last_y & (z < zs - 1))
     def _():
-        pl.semaphore_wait(ready_edge, ys)
         for copy in edges:
             copy.start()
 
@@ -392,25 +437,36 @@
         )
         z_copies.append(copy)
 
+    @pl.when(z == hub - 1)
+    def _():
+        for d in range(1, zs - hub + 1):
+            pl.semaphore_wait(ready_z.at[d - 1], 1)
+
+    for d in range(1, zs - hub + 1):
+        pl.when(z == hub - 1 + d)(z_copies[d - 1].wait_recv)
+    for d in range(1, zs):
+
         @pl.when(z + d < zs)
         def _():
-            pl.semaphore_wait(ready_z.at[d - 1], 1)
-            copy.start()
-
-        pending.append(functools.partial(pl.when(z + d < zs), copy.wait_send))
-
-    own_right[0].wait_recv()
-    on_right = send(6, 6, 0, 4, right)
-    own_left[1].wait_recv()
-    on_left = send(7, 2, 1, 4, left)
-    sib = {(7, 0): send(8, 6, 0, 7, sibling), (3, 1): send(11, 2, 1, 3, sibling)}
+            @pl.when(z < hub - 1)
+            def _():
+                pl.semaphore_wait(ready_z.at[d - 1], 1)
+
+            z_copies[d - 1].start()
+
+        pending.append(functools.partial(pl.when(z + d < zs), z_copies[d - 1].wait_send))
+
+    arrived(0, FACTOR, 0)
+    send(3, FACTOR, 0)
+    arrived(1, FACTOR, 1)
+    send(4, FACTOR, 1)
 
     before[...] = jnp.zeros_like(before)
     for d in range(1, zs):
 
         @pl.when(z >= d)
         def _():
-            z_copies[d - 1].wait_recv()
+            pl.when(z - d != hub - 1)(z_copies[d - 1].wait_recv)
             before[...] += jnp.exp(-float(ROWS * ys * (d - 1)) * rate[:, mine]) * ring_z[d - 1]
 
     sums = before[...]
@@ -448,23 +504,31 @@
                 f_copies[slot, ey] = copy
     flow[0, y] = flow_out[y]
 
-    own_right[1].wait_recv()
-    sib[7, 1] = send(9, 6, 1, 7, sibling)
-    own_left[0].wait_recv()
-    sib[3, 0] = send(10, 2, 0, 3, sibling)
-    on_right.wait_recv()
-    sib[5, 0] = send(12, 4, 0, 5, sibling)
-    on_left.wait_recv()
-    sib[5, 1] = send(13, 4, 1, 5, sibling)
+    arrived(0, OWN, 0)
+    send(3, OWN, 0)
+    arrived(1, OWN, 1)
+    send(4, OWN, 1)
+    send(5, FACTOR, 0)
+    send(6, FACTOR, 1)
+    send(5, OWN, 0)
+    send(6, OWN, 1)
+    for kind in (FACTOR, OWN):
+        arrived(0, kind, 1)
+        send(5, kind, 1)
+        arrived(1, kind, 0)
+        send(6, kind, 0)
+    for kind in (FACTOR, OWN):
+        for p in range(PIECES):
+            arrived(3 + p, kind, p)
+            send(7, kind, p)
 
     loads[8].wait()
     loads[9].wait()
     for n, slot in enumerate((0, 1, 6, 2, 7, 3, 4, 5)):
-        for p in range(PIECES):
-            if slot == 1:
-                own_sib[p].wait_recv()
-            if slot in (3, 5, 7):
-                sib[slot, p].wait_recv()
+        if slot % CORES:
+            for kind in (FACTOR, OWN):
+                for p in range(PIECES):
+                    arrived({1: 2, 7: 5, 3: 6, 5: 7}[slot], kind, p)
         for ey in range(ys):
             if slot or ey:
                 f_copies[slot, ey].wait_recv()
@@ -474,7 +538,7 @@
         )
         blocks = []
         for p in range(PIECES):
-            own, factor = hid[slot, p, 0].astype(F32), hid[slot, p, 1].astype(F32)
+            own, factor = hid[slot, OWN, p].astype(F32), hid[slot, FACTOR, p].astype(F32)
             blocks.append((own + factor * entering[:, p * half : (p + 1) * half]).astype(BF16))
         owner = x_peer(slot // CORES) + (core if slot % CORES == 0 else 1 - core)
         wrows = weight[pl.ds(pl.multiple_of(owner * width, width), width), :]
@@ -536,6 +600,7 @@
         block,
         table,
         block,
+        block,
         pltpu.VMEM((STEPS, width), F32),
         pltpu.VMEM((MODES, STEPS, LANES), F32),
         pltpu.VMEM((tiles, MODES + 16, LANES), F32),
@@ -546,7 +611,7 @@
         tile,
         pltpu.VMEM((ys, STEPS, LANES), BF16),
         pltpu.VMEM((CHIPS * CORES, tiles, STEPS, LANES), BF16),
-        pltpu.VMEM((CHIPS * CORES, PIECES, 2, ROWS, width // PIECES), BF16),
+        pltpu.VMEM((CHIPS * CORES, 2, PIECES, ROWS, width // PIECES), BF16),
         pltpu.VMEM((ROWS, width), F32),
         dma((10,)),
         dma((ys - 1,)),
@@ -555,8 +620,8 @@
         dma,
         dma((zs - 1,)),
         dma((zs - 1,)),
-        dma((14,)),
-        dma((14,)),
+        dma((len(ROUTES), 2, PIECES)),
+        dma((len(ROUTES), 2, PIECES)),
         dma((CHIPS * CORES, ys)),
         dma((CHIPS * CORES, ys)),
         regular,

time: 25 us -> 26.4 us (1.056)
  Pallas kernels: 23.1 us -> 24.6 us
    pallas_call x1, Pallas kernels: 23.1 us -> 24.6 us  [per_device(): pl.pallas_call(functools.partial(kernel, zs, ys), out_shape=jax.ShapeDtyp...]
where the time goes in v4:
time: 26.4 us; the launch traced here: 26.2 us
  Pallas kernels  24.6 us (93%)
  local copies, waits for them, and re-layouts  1.57 us (6%)
    pallas_call x1, Pallas kernels, per_device(): pl.pallas_call(functools.partial(kernel, zs, ys), out_shape=jax.ShapeDtyp...  24.6 us
    unnamed x1, local copies, waits for them, and re-layouts  1.57 us

profile of v4, /device:TPU:225, one launch (start us, length us, event | category | flops | bytes accessed | tf_op | source)
XLA Modules:
  0.0 26.2 jit_solution(10474008121547544150)
XLA Ops:
  0.0 24.6 %shard_map.100 = bf16[128,512]{1,0:T(8,128)(2,1)} custom-call(bf16[128,512]{1,0:T(8,128)(2,1)} %q_hbm.1, bf16[128,512]{1,0:T(8,128)(2,1)} %k_hbm.1, bf16[128,512]{1,0:T(8,128)(2,1)} %v_hbm.1, f32[3,3,512]{2,1,0:T(4,128)} %taps_hbm.1, f32[16,512]{1,0:T(8,128)} %bitcast.3, f32[16,512]{1,0:T(8,128)} %bitcast.4, f32[1,512]{1,0:T(1,128)} %bitcast.5, ...), custom_call_target="tpu_custom_call" | custom-call | tf_op jit(solution)/shard_map/pallas_call | solution.py:632
  24.6 1.6 %copy.12 = bf16[128,512]{1,0:T(8,128)(2,1)} copy(bf16[128,512]{1,0:T(8,128)(2,1)} %shard_map.100) | data formatting | bytes 262144

commit v5 on v3

v5 whole, which is shorter than its diff:
```python
import functools

import jax
import jax.numpy as jnp
import ml_dtypes
import numpy as np
from jax import lax
from jax.experimental import pallas as pl
from jax.experimental.pallas import tpu as pltpu
from jax.sharding import PartitionSpec as P

MESH = pl.DeviceIdType.MESH
F32 = jnp.float32
BF16 = jnp.bfloat16
MODES = 16
STEPS = 16
SUBS = 8
ROWS = STEPS * SUBS
LANES = 128
CHIPS = 4
CORES = 2
PIECES = 2
FACTOR, OWN = 0, 1
ROUTES = (
    (0, 6, "right"),
    (0, 2, "left"),
    (0, 1, "sibling"),
    (6, 4, "right"),
    (2, 4, "left"),
    (6, 7, "sibling"),
    (2, 3, "sibling"),
    (4, 5, "sibling"),
)
NODES = STEPS - 2


def tree_sum(array):
    while array.shape[0] > 1:
        half = array.shape[0] // 2
        array = array[:half] + array[half:]
    return array[0]


def lagged(block, last, last_but_one):
    one = jnp.concatenate([last[None], block[:-1]], axis=0)
    two = jnp.concatenate([last_but_one[None], one[:-1]], axis=0)
    return one, two


def tapped(taps, which, cols, now, one, two):
    return (
        taps[which, 0:1, cols] * now + taps[which, 1:2, cols] * one + taps[which, 2:3, cols] * two
    )


def kernel(
    zs,
    ys,
    q_hbm,
    k_hbm,
    v_hbm,
    taps_hbm,
    res_hbm,
    rate_hbm,
    skip_hbm,
    w_hbm,
    weights_hbm,
    places_hbm,
    out_ref,
    q_in,
    k_in,
    v_in,
    taps,
    res,
    rate,
    skip,
    weight,
    weights,
    places,
    rate3,
    decay3,
    gain3,
    xq,
    xk,
    xv,
    enter,
    local,
    query,
    near,
    node3,
    own_state,
    info,
    edge_z,
    heads,
    starts,
    total,
    half_sum,
    ring_z,
    before,
    flow,
    hid,
    acc,
    load_sem,
    y_send,
    y_recv,
    e_send,
    e_recv,
    z_send,
    z_recv,
    g_send,
    g_recv,
    f_send,
    f_recv,
    ready_z,
    known,
    ready_edge,
):
    seq = lax.axis_index("seq")
    chan = lax.axis_index("chan")
    z, y = seq // ys, lax.rem(seq, ys)
    x, core = chan // CORES, lax.rem(chan, CORES)
    width = k_in.shape[1]
    tiles = width // LANES
    half = width // PIECES
    per = tiles // PIECES
    last_y = y == ys - 1

    loads = [
        pltpu.make_async_copy(src, dst, load_sem.at[i])
        for i, (src, dst) in enumerate(
            [
                (rate_hbm, rate),
                (res_hbm, res),
                (taps_hbm, taps),
                (k_hbm, k_in),
                (v_hbm, v_in),
                (q_hbm, q_in),
                (skip_hbm, skip),
                (places_hbm, places),
                (weights_hbm, weights),
                (w_hbm, weight),
            ]
        )
    ]
    for i in (2, 5, 0, 1, 3, 4, 6, 7, 8, 9):
        loads[i].start()
    pending = []

    def at(zz, yy):
        return zz * ys + yy

    def signal(sem, s, c):
        pl.semaphore_signal(sem, inc=1, device_id=(s, c), device_id_type=MESH)

    def x_peer(e):
        return lax.rem(x + e, CHIPS) * CORES

    right = x_peer(1) + core
    left = x_peer(CHIPS - 1) + core
    sibling = x * CORES + 1 - core
    z_up = lax.rem(z + 1, zs)
    z_down = lax.rem(z + zs - 1, zs)

    barrier = pltpu.get_barrier_semaphore()
    for e in range(1, CHIPS):
        for c in range(CORES):
            signal(barrier, seq, x_peer(e) + c)
    signal(barrier, seq, sibling)
    for e in range(1, ys):
        signal(barrier, at(z, lax.rem(y + e, ys)), chan)
    hub = zs // 2
    early = z < hub
    place = lax.rem(z, hub)
    for d in range(1, zs):

        @pl.when(early & (z + d < zs) & ((z + d < hub) | (z >= hub - 2)))
        def _():
            signal(barrier, at(lax.rem(z + d, zs), y), chan)

    @pl.when((z >= hub) & (z < zs - 1))
    def _():
        signal(barrier, at(z_up, y), chan)

    @pl.when(z > hub)
    def _():
        signal(barrier, at(z_down, y), chan)

    @pl.when(last_y & early)
    def _():
        for e in range(ys):
            signal(barrier, at(z_up, e), chan)

    @pl.when(z > hub)
    def _():
        signal(barrier, at(z_down, ys - 1), chan)

    row = lax.broadcasted_iota(jnp.int32, (ROWS, ROWS), 0)
    col = lax.broadcasted_iota(jnp.int32, (ROWS, ROWS), 1)
    order = jnp.where(col == (row & 7) * STEPS + (row >> 3), 1.0, 0.0).astype(BF16)
    back = jnp.where(row == (col & 7) * STEPS + (col >> 3), 1.0, 0.0).astype(BF16)

    def arranged(block):
        return jnp.dot(order, block, preferred_element_type=F32).reshape(STEPS, SUBS, width)

    sub = lax.broadcasted_iota(jnp.int32, (SUBS, LANES), 0)
    sub3 = lax.broadcasted_iota(jnp.int32, (MODES, SUBS, LANES), 1)
    first = sub == 0
    subf3 = sub3.astype(F32)

    loads[2].wait()
    loads[5].wait()
    xq[...] = arranged(q_in[...])

    pick = lax.broadcasted_iota(jnp.int32, (MODES, ROWS), 0)
    pos = lax.broadcasted_iota(jnp.int32, (MODES, ROWS), 1)

    def ends_of(base, block):
        i = pick - base
        ends = ((i >= 0) & (i < 2) & (pos == i)) | ((i >= 2) & (i < 4) & (pos == i + ROWS - 4))
        return jnp.dot(
            jnp.where(ends, 1.0, 0.0).astype(BF16), block[...], preferred_element_type=F32
        )

    def lags(block):
        last = jnp.where(first, 0.0, pltpu.roll(block[STEPS - 1], 1, 0))
        last_but_one = jnp.where(first, 0.0, pltpu.roll(block[STEPS - 2], 1, 0))
        return lagged(block, last, last_but_one)

    g_copies = {}

    def send(route, kind, piece):
        slot, to_slot, to = ROUTES[route]
        to = {"right": right, "left": left, "sibling": sibling}[to]
        copy = pltpu.make_async_remote_copy(
            hid.at[slot, kind, piece],
            hid.at[to_slot, kind, piece],
            g_send.at[route, kind, piece],
            g_recv.at[route, kind, piece],
            device_id=(seq, to),
            device_id_type=MESH,
        )
        copy.start()
        pending.append(copy.wait_send)
        g_copies[route, kind, piece] = copy

    def arrived(route, kind, piece):
        g_copies[route, kind, piece].wait_recv()

    for l in range(tiles):
        cols = slice(l * LANES, (l + 1) * LANES)
        qb = xq[:, :, cols]
        qb = tapped(taps, 0, cols, qb, *lags(qb))
        query[:, :, cols] = qb
        qb = jnp.concatenate([jnp.where(first[None], 1.0, qb[:2]), qb[2:]], axis=0)
        to = slice(l % per * LANES, (l % per + 1) * LANES)
        hid[0, FACTOR, l // per, :, to] = qb.reshape(ROWS, LANES).astype(BF16)
    pl.semaphore_wait(
        barrier,
        (CORES * CHIPS - 1 + ys - 1)
        + jnp.where(early, z, 2 + jnp.where(z > hub, 1, 0) + jnp.where(z < zs - 1, 1, 0))
        + jnp.where((z > 0) & (z <= hub), 1, 0)
        + jnp.where(last_y & (z >= hub) & (z < zs - 1), ys, 0),
    )
    for d in range(1, zs):

        @pl.when((z >= d) & (z - d < hub) & (early | (z - d >= hub - 2)))
        def _():
            signal(ready_z.at[d - 1], at(lax.rem(z + zs - d, zs), y), chan)

    @pl.when((z > hub) & (z < zs - 1))
    def _():
        signal(known.at[0], at(z_down, y), chan)

    @pl.when((z > 0) & (z <= hub))
    def _():
        signal(ready_edge, at(z_down, ys - 1), chan)

    for route, piece in ((0, 0), (1, 1), (0, 1), (1, 0), (2, 0), (2, 1)):
        send(route, FACTOR, piece)

    loads[0].wait()
    loads[1].wait()
    r = rate[...]
    series = r * (1.0 - r * (1 / 2) * (1.0 - r * (1 / 3) * (1.0 - r * (1 / 4) * (1.0 - r * (1 / 5) * (1.0 - r * (1 / 6))))))
    gain = res[...] * series
    decay = jnp.exp(-r)
    for m in range(MODES):
        rate3[m] = jnp.broadcast_to(r[m : m + 1], (SUBS, width))
        decay3[m] = jnp.broadcast_to(decay[m : m + 1], (SUBS, width))
        gain3[m] = jnp.broadcast_to(gain[m : m + 1], (SUBS, width))

    loads[3].wait()
    loads[4].wait()
    xk[...] = arranged(k_in[...])
    xv[...] = arranged(v_in[...])
    info[y, MODES : MODES + 16, :] = (ends_of(0, k_in) + ends_of(4, v_in) + ends_of(8, q_in)).astype(BF16)
    for l in range(tiles):
        cols = slice(l * LANES, (l + 1) * LANES)
        kb, vb = xk[:, :, cols], xv[:, :, cols]
        g = tapped(taps, 1, cols, kb, *lags(kb)) * tapped(taps, 2, cols, vb, *lags(vb))
        g = jnp.concatenate([jnp.where(first[None], 0.0, g[:2]), g[2:]], axis=0)
        local[:, :, cols] = g
        a = decay3[:, :, cols]
        state = jnp.broadcast_to(g[0][None], a.shape)
        for j in range(1, STEPS):
            state = state * a + g[j][None]
        step = a
        for _ in range(4):
            step = step * step
        for reach in (1, 2, 4):
            state = state + jnp.where(sub3 >= reach, step, 0.0) * pltpu.roll(state, reach, 1)
            step = step * step
        enter[:, :, cols] = jnp.where(sub3 >= 1, pltpu.roll(state, 1, 1), 0.0)
        for m in range(MODES):
            own_state[m : m + 1, cols] = state[m, SUBS - 1 : SUBS, :]

    info[y, 0:MODES, :] = own_state[...].astype(BF16)

    y_copies = []
    for e in range(1, ys):
        copy = pltpu.make_async_remote_copy(
            info.at[y], info.at[y], y_send.at[e - 1], y_recv.at[e - 1],
            device_id=(at(z, lax.rem(y + e, ys)), chan), device_id_type=MESH,
        )
        copy.start()
        pending.append(copy.wait_send)
        y_copies.append(copy)

    loads[6].wait()
    for p in range(PIECES):
        for i in range(per):
            l = p * per + i
            cols = slice(l * LANES, (l + 1) * LANES)
            r3, a, w = rate3[:, :, cols], decay3[:, :, cols], gain3[:, :, cols]
            close = w * jnp.exp(-subf3 * r3)
            a8 = a * a
            a8 = a8 * a8
            a8 = a8 * a8
            near[0:SUBS, cols] = tree_sum(close)
            near[SUBS : 2 * SUBS, cols] = tree_sum(close * a8)
            g = local[:, :, cols]
            out = g * skip[0:1, cols]
            for d in range(STEPS):
                add = g[: STEPS - d] * near[d : d + 1, cols][None]
                out = out + add if d == 0 else jnp.concatenate([out[:d], out[d:] + add], axis=0)
            state = w * a * enter[:, :, cols]
            own = []
            for j in range(STEPS):
                line = query[j, :, cols] * (out[j] + tree_sum(state))
                if j < STEPS - 1:
                    state = state * a
                own.append(jnp.where(first, 0.0, line) if j < 2 else line)
            to = slice(i * LANES, (i + 1) * LANES)
            hid[0, OWN, p, :, to] = jnp.concatenate(own, axis=0).astype(BF16)
        send(0, OWN, p)
        send(2, OWN, p)
    for p in reversed(range(PIECES)):
        send(1, OWN, p)

    edges = [
        pltpu.make_async_remote_copy(
            info.at[y, pl.ds(MODES, 16)], edge_z, e_send.at[e], e_recv,
            device_id=(at(z_up, e), chan), device_id_type=MESH,
        )
        for e in range(ys)
    ]

    @pl.when(last_y & early)
    def _():
        pl.semaphore_wait(ready_edge, ys)

    @pl.when(last_y & (z < zs - 1))
    def _():
        for copy in edges:
            copy.start()

    @pending.append
    def _():
        @pl.when(last_y & (z < zs - 1))
        def _():
            for copy in edges:
                copy.wait_send()

    for i in range(hub - 2):

        @pl.when((z >= hub) & (z + 2 + i < zs))
        def _():
            pl.semaphore_wait(known.at[i], 1)
            if i < hub - 3:
                pl.when(z > hub)(lambda: signal(known.at[i + 1], at(z_down, y), chan))

    arrived(0, FACTOR, 0)
    send(3, FACTOR, 0)
    arrived(1, FACTOR, 1)
    send(4, FACTOR, 1)

    r = rate[...]
    a126 = jnp.exp(-(ROWS - 2.0) * r)
    a127 = jnp.exp(-(ROWS - 1.0) * r)
    a128 = jnp.exp(-float(ROWS) * r)
    everything = slice(0, width)
    loads[7].wait()
    for l in range(tiles):
        cols = slice(l * LANES, (l + 1) * LANES)
        for m in range(MODES):
            node3[m, :, cols] = gain3[m, 0:1, cols] * jnp.exp(
                -(places[...] + 1.0) * rate[m : m + 1, cols]
            )

    @pl.when(z == 0)
    def _():
        edge_z[...] = jnp.zeros_like(edge_z)

    @pl.when(z > 0)
    def _():
        edges[0].wait_recv()

    for copy in y_copies:
        copy.wait_recv()
    ends = edge_z[...].astype(F32)
    start = jnp.zeros_like(r)
    for e in range(ys):
        now = info[e, MODES : MODES + 16, :].astype(F32)
        k0, k1, v0, v1 = (now[i : i + 1] for i in (0, 1, 4, 5))
        k126, k127, v126, v127, q126, q127 = (ends[i : i + 1] for i in (2, 3, 6, 7, 10, 11))
        g0 = tapped(taps, 1, everything, k0, k127, k126) * tapped(
            taps, 2, everything, v0, v127, v126
        )
        g1 = tapped(taps, 1, everything, k1, k0, k127) * tapped(taps, 2, everything, v1, v0, v127)
        for i, line in enumerate((g0, g1, q126, q127)):
            heads[e, i : i + 1, :] = line
        starts[e] = start
        start = start * a128 + (info[e, 0:MODES, :].astype(F32) + a127 * g0 + a126 * g1)
        ends = now
    total[...] = start.astype(BF16)

    to_half = hub - z

    def to_later(source, d):
        return pltpu.make_async_remote_copy(
            source, ring_z.at[d - 1], z_send.at[d - 1], z_recv.at[d - 1],
            device_id=(at(lax.rem(z + d, zs), y), chan), device_id_type=MESH,
        )

    def send_sums(source, distances, which):
        for d in distances:

            @pl.when((z + d < zs) & which(d))
            def _():
                @pl.when(early)
                def _():
                    pl.semaphore_wait(ready_z.at[d - 1], 1)

                to_later(source, d).start()

            pending.append(
                functools.partial(
                    pl.when((z + d < zs) & which(d)), to_later(source, d).wait_send
                )
            )

    send_sums(total, range(hub - 1, 0, -1), lambda d: (z >= hub) | (d < to_half))
    send_sums(total, range(hub, 0, -1), lambda d: z == hub - 1)

    arrived(0, OWN, 0)
    send(3, OWN, 0)
    arrived(1, OWN, 1)
    send(4, OWN, 1)
    send(5, FACTOR, 0)
    send(6, FACTOR, 1)
    arrived(0, FACTOR, 1)
    send(5, FACTOR, 1)
    arrived(1, FACTOR, 0)
    send(6, FACTOR, 0)
    before[...] = jnp.zeros_like(before)
    for d in range(1, hub + 2):

        @pl.when((z >= d) & (early | (z - d >= hub - 2)))
        def _():
            to_later(total, d).wait_recv()
            before[...] += (
                jnp.exp(-float(ROWS * ys * (d - 1)) * rate[...]) * ring_z[d - 1].astype(F32)
            )

    @pl.when(z == hub - 2)
    def _():
        half_sum[...] = (
            total[...].astype(F32) + jnp.exp(-float(ROWS * ys) * rate[...]) * before[...]
        ).astype(BF16)

    send_sums(half_sum, range(hub + 1, 1, -1), lambda d: z == hub - 2)

    entering = starts[y] + jnp.exp(-float(ROWS) * y.astype(F32) * r) * before[...]
    g0, g1, q126, q127 = (heads[y, i : i + 1, :] for i in range(4))
    later = entering + jnp.exp(r) * g0 + jnp.exp(2.0 * r) * g1
    rows = lax.broadcasted_iota(jnp.int32, (STEPS, LANES), 0)
    now = info[y, MODES : MODES + 16, :].astype(F32)
    s0 = tapped(taps, 0, everything, now[8:9], q127, q126)
    s1 = tapped(taps, 0, everything, now[9:10], now[8:9], q127)
    for l in range(tiles):
        cols = slice(l * LANES, (l + 1) * LANES)
        near0, near1, direct = near[0:1, cols], near[1:2, cols], skip[0:1, cols]
        values = jnp.zeros((STEPS, LANES), F32)
        for m in range(MODES):
            values += node3[m, :, cols] * jnp.where(
                rows < NODES, later[m : m + 1, cols], entering[m : m + 1, cols]
            )
        c0, c1 = g0[:, cols], g1[:, cols]
        h0 = s0[:, cols] * (values[NODES : NODES + 1] + (near0 + direct) * c0)
        h1 = s1[:, cols] * (values[NODES + 1 : NODES + 2] + near1 * c0 + (near0 + direct) * c1)
        values = jnp.where(rows == NODES, h0, jnp.where(rows == NODES + 1, h1, values))
        flow[0, :, cols] = values.astype(BF16)

    f_copies = {}
    for ex in (2, 1, 3, 0):
        for ec in range(CORES):
            slot = ex * CORES + ec
            if slot:
                to = x_peer(CHIPS - ex) + (core if ec == 0 else 1 - core)
                copy = pltpu.make_async_remote_copy(
                    flow.at[0], flow.at[slot], f_send.at[slot], f_recv.at[slot],
                    device_id=(seq, to), device_id_type=MESH,
                )
                copy.start()
                pending.append(copy.wait_send)
                f_copies[slot] = copy

    send(5, OWN, 0)
    send(6, OWN, 1)
    arrived(0, OWN, 1)
    send(5, OWN, 1)
    arrived(1, OWN, 0)
    send(6, OWN, 0)
    for kind in (FACTOR, OWN):
        for p in range(PIECES):
            arrived(3 + p, kind, p)
            send(7, kind, p)

    loads[8].wait()
    loads[9].wait()
    for n, slot in enumerate((0, 1, 6, 2, 7, 3, 4, 5)):
        if slot % CORES:
            for kind in (FACTOR, OWN):
                for p in range(PIECES):
                    arrived({1: 2, 7: 5, 3: 6, 5: 7}[slot], kind, p)
        if slot:
            f_copies[slot].wait_recv()
        values = flow[slot]
        entering = jnp.dot(
            weights[...], jnp.concatenate([values, values], axis=0), preferred_element_type=F32
        )
        blocks = []
        for p in range(PIECES):
            own, factor = hid[slot, OWN, p].astype(F32), hid[slot, FACTOR, p].astype(F32)
            blocks.append((own + factor * entering[:, p * half : (p + 1) * half]).astype(BF16))
        owner = x_peer(slot // CORES) + (core if slot % CORES == 0 else 1 - core)
        wrows = weight[pl.ds(pl.multiple_of(owner * width, width), width), :]
        part = jnp.dot(jnp.concatenate(blocks, axis=1), wrows, preferred_element_type=F32)
        if n:
            part = part + acc[...]
        acc[...] = part

    mixed = acc[...].astype(BF16)
    out_ref[...] = jnp.dot(back, mixed, preferred_element_type=F32).astype(BF16)

    for wait in pending:
        wait()


def interpolation():
    turn = np.pi * (2 * np.arange(NODES) + 1) / (2 * NODES)
    places = ((ROWS - 1) / 2 * (1 - np.cos(turn))).astype(np.float32)
    at = places.astype(np.float64)
    share = np.array([1 / np.prod(at[i] - np.delete(at, i)) for i in range(NODES)])
    weights = np.zeros((ROWS, STEPS))
    for t in range(2, ROWS):
        part = share / (t - at)
        weights[t, :NODES] = part / part.sum()
    weights[0, NODES] = weights[1, NODES + 1] = 1
    weights = weights.reshape(SUBS, STEPS, STEPS).swapaxes(0, 1).reshape(ROWS, STEPS)
    high = weights.astype(ml_dtypes.bfloat16)
    low = (weights - high.astype(np.float64)).astype(ml_dtypes.bfloat16)
    places = np.broadcast_to(np.append(places, [0, 1]).astype(np.float32)[:, None], (STEPS, LANES))
    return np.concatenate([high, low], axis=1), np.ascontiguousarray(places)


def per_device(zs, ys, query, key, value, short_taps, residue, rate, skip, out_weight):
    width = query.shape[1]
    tiles = width // LANES
    weights, places = interpolation()
    modes = pltpu.VMEM((MODES, width), F32)
    table = pltpu.VMEM((MODES, SUBS, width), F32)
    block = pltpu.VMEM((STEPS, SUBS, width), F32)
    dma = pltpu.SemaphoreType.DMA
    regular = pltpu.SemaphoreType.REGULAR
    scratch = [
        pltpu.VMEM((ROWS, width), BF16),
        pltpu.VMEM((ROWS, width), BF16),
        pltpu.VMEM((ROWS, width), BF16),
        pltpu.VMEM(short_taps.shape, F32),
        modes,
        modes,
        pltpu.VMEM((1, width), F32),
        pltpu.VMEM(out_weight.shape, BF16),
        pltpu.VMEM(weights.shape, BF16),
        pltpu.VMEM(places.shape, F32),
        table,
        table,
        table,
        block,
        block,
        block,
        table,
        block,
        block,
        pltpu.VMEM((STEPS, width), F32),
        pltpu.VMEM((MODES, STEPS, width), F32),
        modes,
        pltpu.VMEM((ys, MODES + 16, width), BF16),
        pltpu.VMEM((16, width), BF16),
        pltpu.VMEM((ys, 8, width), F32),
        pltpu.VMEM((ys, MODES, width), F32),
        pltpu.VMEM((MODES, width), BF16),
        pltpu.VMEM((MODES, width), BF16),
        pltpu.VMEM((zs - 1, MODES, width), BF16),
        modes,
        pltpu.VMEM((CHIPS * CORES, STEPS, width), BF16),
        pltpu.VMEM((CHIPS * CORES, 2, PIECES, ROWS, width // PIECES), BF16),
        pltpu.VMEM((ROWS, width), F32),
        dma((10,)),
        dma((ys - 1,)),
        dma((ys - 1,)),
        dma((ys,)),
        dma,
        dma((zs - 1,)),
        dma((zs - 1,)),
        dma((len(ROUTES), 2, PIECES)),
        dma((len(ROUTES), 2, PIECES)),
        dma((CHIPS * CORES,)),
        dma((CHIPS * CORES,)),
        regular((zs - 1,)),
        regular((zs // 2 - 2,)),
        regular,
    ]
    return pl.pallas_call(
        functools.partial(kernel, zs, ys),
        out_shape=jax.ShapeDtypeStruct((ROWS, width), BF16),
        in_specs=[pl.BlockSpec(memory_space=pl.ANY)] * 10,
        out_specs=pl.BlockSpec(memory_space=pltpu.VMEM),
        scratch_shapes=scratch,
        compiler_params=pltpu.CompilerParams(
            collective_id=0, has_side_effects=True, vmem_limit_bytes=56 * 1024 * 1024
        ),
    )(
        query,
        key,
        value,
        short_taps,
        residue.T,
        rate.T,
        skip[None, :],
        out_weight,
        jnp.asarray(weights),
        jnp.asarray(places),
    )


def solution(mesh, ys=4):
    placed = (
        P("seq", "chan"),
        P("seq", "chan"),
        P("seq", "chan"),
        P(None, None, "chan"),
        P("chan", None),
        P("chan", None),
        P("chan"),
        P(None, "chan"),
    )
    return jax.shard_map(
        functools.partial(per_device, mesh.shape["seq"] // ys, ys),
        mesh=mesh,
        in_specs=placed,
        out_specs=P("seq", "chan"),
        check_vma=False,
    )
```

time: 25 us -> 24.2 us (0.968); the launches traced: 24.6 us -> 24.2 us
  Pallas kernels: 23.1 us -> 22.6 us
    pallas_call x1, Pallas kernels: 23.1 us -> 22.6 us  [per_device(): pl.pallas_call(functools.partial(kernel, zs, ys), out_shape=jax.ShapeDtyp...]
where the time goes in v5:
time: 24.2 us
  Pallas kernels  22.6 us (93%)
  local copies, waits for them, and re-layouts  1.57 us (6%)
    pallas_call x1, Pallas kernels, per_device(): pl.pallas_call(functools.partial(kernel, zs, ys), out_shape=jax.ShapeDtyp...  22.6 us
    unnamed x1, local copies, waits for them, and re-layouts  1.57 us

profile of v5, /device:TPU:225, one launch (start us, length us, event | category | flops | bytes accessed | tf_op | source)
XLA Modules:
  0.0 24.2 jit_solution(8488855028201562245)
XLA Ops:
  0.0 22.6 %shard_map.100 = bf16[128,512]{1,0:T(8,128)(2,1)} custom-call(bf16[128,512]{1,0:T(8,128)(2,1)} %q_hbm.1, bf16[128,512]{1,0:T(8,128)(2,1)} %k_hbm.1, bf16[128,512]{1,0:T(8,128)(2,1)} %v_hbm.1, f32[3,3,512]{2,1,0:T(4,128)} %taps_hbm.1, f32[16,512]{1,0:T(8,128)} %bitcast.3, f32[16,512]{1,0:T(8,128)} %bitcast.4, f32[1,512]{1,0:T(1,128)} %bitcast.5, ...), custom_call_target="tpu_custom_call" | custom-call | tf_op jit(solution)/shard_map/pallas_call | solution.py:645
  22.6 1.6 %copy.12 = bf16[128,512]{1,0:T(8,128)(2,1)} copy(bf16[128,512]{1,0:T(8,128)(2,1)} %shard_map.100) | data formatting | bytes 262144

commit v6 on v5

--- a/solution.py
+++ b/solution.py
@@ -90,7 +90,7 @@
     node3,
     own_state,
     info,
-    edge_z,
+    ends_before,
     heads,
     starts,
     total,
@@ -103,8 +103,6 @@
     load_sem,
     y_send,
     y_recv,
-    e_send,
-    e_recv,
     z_send,
     z_recv,
     g_send,
@@ -113,7 +111,6 @@
     f_recv,
     ready_z,
     known,
-    ready_edge,
 ):
     seq = lax.axis_index("seq")
     chan = lax.axis_index("chan")
@@ -123,7 +120,6 @@
     tiles = width // LANES
     half = width // PIECES
     per = tiles // PIECES
-    last_y = y == ys - 1
 
     loads = [
         pltpu.make_async_copy(src, dst, load_sem.at[i])
@@ -185,15 +181,6 @@
     def _():
         signal(barrier, at(z_down, y), chan)
 
-    @pl.when(last_y & early)
-    def _():
-        for e in range(ys):
-            signal(barrier, at(z_up, e), chan)
-
-    @pl.when(z > hub)
-    def _():
-        signal(barrier, at(z_down, ys - 1), chan)
-
     row = lax.broadcasted_iota(jnp.int32, (ROWS, ROWS), 0)
     col = lax.broadcasted_iota(jnp.int32, (ROWS, ROWS), 1)
     order = jnp.where(col == (row & 7) * STEPS + (row >> 3), 1.0, 0.0).astype(BF16)
@@ -258,8 +245,6 @@
         barrier,
         (CORES * CHIPS - 1 + ys - 1)
         + jnp.where(early, z, 2 + jnp.where(z > hub, 1, 0) + jnp.where(z < zs - 1, 1, 0))
-        + jnp.where((z > 0) & (z <= hub), 1, 0)
-        + jnp.where(last_y & (z >= hub) & (z < zs - 1), ys, 0),
     )
     for d in range(1, zs):
 
@@ -270,10 +255,6 @@
     @pl.when((z > hub) & (z < zs - 1))
     def _():
         signal(known.at[0], at(z_down, y), chan)
-
-    @pl.when((z > 0) & (z <= hub))
-    def _():
-        signal(ready_edge, at(z_down, ys - 1), chan)
 
     for route, piece in ((0, 0), (1, 1), (0, 1), (1, 0), (2, 0), (2, 1)):
         send(route, FACTOR, piece)
@@ -357,30 +338,6 @@
     for p in reversed(range(PIECES)):
         send(1, OWN, p)
 
-    edges = [
-        pltpu.make_async_remote_copy(
-            info.at[y, pl.ds(MODES, 16)], edge_z, e_send.at[e], e_recv,
-            device_id=(at(z_up, e), chan), device_id_type=MESH,
-        )
-        for e in range(ys)
-    ]
-
-    @pl.when(last_y & early)
-    def _():
-        pl.semaphore_wait(ready_edge, ys)
-
-    @pl.when(last_y & (z < zs - 1))
-    def _():
-        for copy in edges:
-            copy.start()
-
-    @pending.append
-    def _():
-        @pl.when(last_y & (z < zs - 1))
-        def _():
-            for copy in edges:
-                copy.wait_send()
-
     for i in range(hub - 2):
 
         @pl.when((z >= hub) & (z + 2 + i < zs))
@@ -407,32 +364,39 @@
                 -(places[...] + 1.0) * rate[m : m + 1, cols]
             )
 
-    @pl.when(z == 0)
-    def _():
-        edge_z[...] = jnp.zeros_like(edge_z)
-
-    @pl.when(z > 0)
-    def _():
-        edges[0].wait_recv()
-
     for copy in y_copies:
         copy.wait_recv()
-    ends = edge_z[...].astype(F32)
-    start = jnp.zeros_like(r)
-    for e in range(ys):
-        now = info[e, MODES : MODES + 16, :].astype(F32)
+    a384 = jnp.exp(-float(ROWS * (ys - 1)) * r)
+    a512 = jnp.exp(-float(ROWS * ys) * r)
+
+    def first_two(now, ends):
         k0, k1, v0, v1 = (now[i : i + 1] for i in (0, 1, 4, 5))
-        k126, k127, v126, v127, q126, q127 = (ends[i : i + 1] for i in (2, 3, 6, 7, 10, 11))
+        k126, k127, v126, v127 = (ends[i : i + 1] for i in (2, 3, 6, 7))
         g0 = tapped(taps, 1, everything, k0, k127, k126) * tapped(
             taps, 2, everything, v0, v127, v126
         )
         g1 = tapped(taps, 1, everything, k1, k0, k127) * tapped(taps, 2, everything, v1, v0, v127)
-        for i, line in enumerate((g0, g1, q126, q127)):
+        return g0, g1
+
+    def set_heads(e, now, ends):
+        g0, g1 = first_two(now, ends)
+        for i, line in enumerate((g0, g1, ends[10:11], ends[11:12])):
             heads[e, i : i + 1, :] = line
+        return a127 * g0 + a126 * g1
+
+    firsts = info[0, MODES : MODES + 16, :].astype(F32)
+    ends = firsts
+    starts[0] = jnp.zeros_like(r)
+    start = info[0, 0:MODES, :].astype(F32)
+    for e in range(1, ys):
+        now = info[e, MODES : MODES + 16, :].astype(F32)
         starts[e] = start
-        start = start * a128 + (info[e, 0:MODES, :].astype(F32) + a127 * g0 + a126 * g1)
+        start = start * a128 + (info[e, 0:MODES, :].astype(F32) + set_heads(e, now, ends))
         ends = now
-    total[...] = start.astype(BF16)
+    total[0:MODES, :] = start.astype(BF16)
+    line = lax.broadcasted_iota(jnp.int32, (16, width), 0)
+    rows_of_group = jnp.where((line & 3) < 2, firsts, ends)
+    total[MODES : MODES + 16, :] = rows_of_group.astype(BF16)
 
     to_half = hub - z
 
@@ -473,24 +437,32 @@
     arrived(1, FACTOR, 0)
     send(6, FACTOR, 0)
     before[...] = jnp.zeros_like(before)
-    for d in range(1, hub + 2):
+    ends_before[...] = jnp.zeros_like(ends_before)
+    for d in range(hub + 1, 0, -1):
 
         @pl.when((z >= d) & (early | (z - d >= hub - 2)))
         def _():
             to_later(total, d).wait_recv()
-            before[...] += (
-                jnp.exp(-float(ROWS * ys * (d - 1)) * rate[...]) * ring_z[d - 1].astype(F32)
-            )
+            now = ring_z[d - 1, MODES : MODES + 16, :].astype(F32)
+            g0, g1 = first_two(now, ends_before[...])
+            head = jnp.where(early | (z - d > hub - 2), 1.0, 0.0) * (a127 * g0 + a126 * g1)
+            arrived_sum = ring_z[d - 1, 0:MODES, :].astype(F32) + a384 * head
+            before[...] = before[...] * a512 + arrived_sum
+            ends_before[...] = now
+
+    head = set_heads(0, firsts, ends_before[...])
 
     @pl.when(z == hub - 2)
     def _():
-        half_sum[...] = (
-            total[...].astype(F32) + jnp.exp(-float(ROWS * ys) * rate[...]) * before[...]
-        ).astype(BF16)
+        whole = total[0:MODES, :].astype(F32) + a384 * head + a512 * before[...]
+        half_sum[0:MODES, :] = whole.astype(BF16)
+        half_sum[MODES : MODES + 16, :] = total[MODES : MODES + 16, :]
 
     send_sums(half_sum, range(hub + 1, 1, -1), lambda d: z == hub - 2)
 
     entering = starts[y] + jnp.exp(-float(ROWS) * y.astype(F32) * r) * before[...]
+    since = jnp.maximum(y - 1, 0).astype(F32)
+    entering = entering + jnp.where(y > 0, jnp.exp(-float(ROWS) * since * r) * head, 0.0)
     g0, g1, q126, q127 = (heads[y, i : i + 1, :] for i in range(4))
     later = entering + jnp.exp(r) * g0 + jnp.exp(2.0 * r) * g1
     rows = lax.broadcasted_iota(jnp.int32, (STEPS, LANES), 0)
@@ -617,12 +589,12 @@
         pltpu.VMEM((MODES, STEPS, width), F32),
         modes,
         pltpu.VMEM((ys, MODES + 16, width), BF16),
-        pltpu.VMEM((16, width), BF16),
+        pltpu.VMEM((16, width), F32),
         pltpu.VMEM((ys, 8, width), F32),
         pltpu.VMEM((ys, MODES, width), F32),
-        pltpu.VMEM((MODES, width), BF16),
-        pltpu.VMEM((MODES, width), BF16),
-        pltpu.VMEM((zs - 1, MODES, width), BF16),
+        pltpu.VMEM((MODES + 16, width), BF16),
+        pltpu.VMEM((MODES + 16, width), BF16),
+        pltpu.VMEM((zs - 1, MODES + 16, width), BF16),
         modes,
         pltpu.VMEM((CHIPS * CORES, STEPS, width), BF16),
         pltpu.VMEM((CHIPS * CORES, 2, PIECES, ROWS, width // PIECES), BF16),
@@ -630,8 +602,6 @@
         dma((10,)),
         dma((ys - 1,)),
         dma((ys - 1,)),
-        dma((ys,)),
-        dma,
         dma((zs - 1,)),
         dma((zs - 1,)),
         dma((len(ROUTES), 2, PIECES)),
@@ -640,7 +610,6 @@
         dma((CHIPS * CORES,)),
         regular((zs - 1,)),
         regular((zs // 2 - 2,)),
-        regular,
     ]
     return pl.pallas_call(
         functools.partial(kernel, zs, ys),

time: 24.2 us -> 23.7 us (0.979)
  the two profiles are of different devices: /device:TPU:225 before, /device:TPU:160 now
where the time goes in v6:
time: 23.7 us; the launch traced here: 23.6 us
  Pallas kernels  22 us (93%)
  local copies, waits for them, and re-layouts  1.57 us (7%)
    pallas_call x1, Pallas kernels, per_device(): pl.pallas_call(functools.partial(kernel, zs, ys), out_shape=jax.ShapeDtyp...  22 us
    unnamed x1, local copies, waits for them, and re-layouts  1.57 us

profile of v6, /device:TPU:160, one launch (start us, length us, event | category | flops | bytes accessed | tf_op | source)
XLA Modules:
  0.0 23.6 jit_solution(12071181458445707147)
XLA Ops:
  0.0 22.0 %shard_map.100 = bf16[128,512]{1,0:T(8,128)(2,1)} custom-call(bf16[128,512]{1,0:T(8,128)(2,1)} %q_hbm.1, bf16[128,512]{1,0:T(8,128)(2,1)} %k_hbm.1, bf16[128,512]{1,0:T(8,128)(2,1)} %v_hbm.1, f32[3,3,512]{2,1,0:T(4,128)} %taps_hbm.1, f32[16,512]{1,0:T(8,128)} %bitcast.3, f32[16,512]{1,0:T(8,128)} %bitcast.4, f32[1,512]{1,0:T(1,128)} %bitcast.5, ...), custom_call_target="tpu_custom_call" | custom-call | tf_op jit(solution)/shard_map/pallas_call | solution.py:614
  22.0 1.6 %copy.12 = bf16[128,512]{1,0:T(8,128)(2,1)} copy(bf16[128,512]{1,0:T(8,128)(2,1)} %shard_map.100) | data formatting | bytes 262144

commit v7 on v6

--- a/solution.py
+++ b/solution.py
@@ -613,7 +613,7 @@
     ]
     return pl.pallas_call(
         functools.partial(kernel, zs, ys),
-        out_shape=jax.ShapeDtypeStruct((ROWS, width), BF16),
+        out_shape=pltpu.VMEM((ROWS, width), BF16),
         in_specs=[pl.BlockSpec(memory_space=pl.ANY)] * 10,
         out_specs=pl.BlockSpec(memory_space=pltpu.VMEM),
         scratch_shapes=scratch,

time: 23.7 us -> 22.1 us (0.932)
  local copies, waits for them, and re-layouts: 1.57 us -> 0.66 us
  Pallas kernels: 22 us -> 21.3 us
    unnamed x1, local copies, waits for them, and re-layouts: 1.57 us -> 0.66 us
    pallas_call x1, Pallas kernels: 22 us -> 21.3 us  [per_device(): pl.pallas_call(functools.partial(kernel, zs, ys), out_shape=pltpu.VMEM((R...]
where the time goes in v7:
time: 22.1 us; the launch traced here: 22 us
  Pallas kernels  21.3 us (96%)
  local copies, waits for them, and re-layouts  0.66 us (3%)
    pallas_call x1, Pallas kernels, per_device(): pl.pallas_call(functools.partial(kernel, zs, ys), out_shape=pltpu.VMEM((R...  21.3 us
    unnamed x1, local copies, waits for them, and re-layouts  0.66 us

profile of v7, /device:TPU:160, one launch (start us, length us, event | category | flops | bytes accessed | tf_op | source)
XLA Modules:
  0.0 22.0 jit_solution(11178476284899808351)
XLA Ops:
  0.0 21.3 %shard_map.100 = bf16[128,512]{1,0:T(8,128)(2,1)S(1)} custom-call(bf16[128,512]{1,0:T(8,128)(2,1)} %q_hbm.1, bf16[128,512]{1,0:T(8,128)(2,1)} %k_hbm.1, bf16[128,512]{1,0:T(8,128)(2,1)} %v_hbm.1, f32[3,3,512]{2,1,0:T(4,128)} %taps_hbm.1, f32[16,512]{1,0:T(8,128)} %bitcast.3, f32[16,512]{1,0:T(8,128)} %bitcast.4, f32[1,512]{1,0:T(1,128)} %bitcast.5, ...), custom_call_target="tpu_custom_call" | custom-call | tf_op jit(solution)/shard_map/pallas_call | solution.py:614
  21.3 0.7 %copy.12 = bf16[128,512]{1,0:T(8,128)(2,1)} copy(bf16[128,512]{1,0:T(8,128)(2,1)S(1)} %shard_map.100) | data formatting | bytes 262144

commit v8 on v7

--- a/solution.py
+++ b/solution.py
@@ -241,6 +241,10 @@
         qb = jnp.concatenate([jnp.where(first[None], 1.0, qb[:2]), qb[2:]], axis=0)
         to = slice(l % per * LANES, (l % per + 1) * LANES)
         hid[0, FACTOR, l // per, :, to] = qb.reshape(ROWS, LANES).astype(BF16)
+    loads[3].wait()
+    loads[4].wait()
+    info[y, MODES : MODES + 16, :] = (ends_of(0, k_in) + ends_of(4, v_in) + ends_of(8, q_in)).astype(BF16)
+
     pl.semaphore_wait(
         barrier,
         (CORES * CHIPS - 1 + ys - 1)
@@ -256,9 +260,29 @@
     def _():
         signal(known.at[0], at(z_down, y), chan)
 
+    def to_group(part):
+        copies = []
+        for e in range(1, ys):
+            copy = pltpu.make_async_remote_copy(
+                info.at[y, pl.ds(MODES * part, MODES)],
+                info.at[y, pl.ds(MODES * part, MODES)],
+                y_send.at[part, e - 1],
+                y_recv.at[part, e - 1],
+                device_id=(at(z, lax.rem(y + e, ys)), chan),
+                device_id_type=MESH,
+            )
+            copy.start()
+            pending.append(copy.wait_send)
+            copies.append(copy)
+        return copies
+
+    row_copies = to_group(1)
+
     for route, piece in ((0, 0), (1, 1), (0, 1), (1, 0), (2, 0), (2, 1)):
         send(route, FACTOR, piece)
 
+    xk[...] = arranged(k_in[...])
+    xv[...] = arranged(v_in[...])
     loads[0].wait()
     loads[1].wait()
     r = rate[...]
@@ -270,11 +294,6 @@
         decay3[m] = jnp.broadcast_to(decay[m : m + 1], (SUBS, width))
         gain3[m] = jnp.broadcast_to(gain[m : m + 1], (SUBS, width))
 
-    loads[3].wait()
-    loads[4].wait()
-    xk[...] = arranged(k_in[...])
-    xv[...] = arranged(v_in[...])
-    info[y, MODES : MODES + 16, :] = (ends_of(0, k_in) + ends_of(4, v_in) + ends_of(8, q_in)).astype(BF16)
     for l in range(tiles):
         cols = slice(l * LANES, (l + 1) * LANES)
         kb, vb = xk[:, :, cols], xv[:, :, cols]
@@ -297,15 +316,7 @@
 
     info[y, 0:MODES, :] = own_state[...].astype(BF16)
 
-    y_copies = []
-    for e in range(1, ys):
-        copy = pltpu.make_async_remote_copy(
-            info.at[y], info.at[y], y_send.at[e - 1], y_recv.at[e - 1],
-            device_id=(at(z, lax.rem(y + e, ys)), chan), device_id_type=MESH,
-        )
-        copy.start()
-        pending.append(copy.wait_send)
-        y_copies.append(copy)
+    y_copies = to_group(0)
 
     loads[6].wait()
     for p in range(PIECES):
@@ -346,6 +357,45 @@
             if i < hub - 3:
                 pl.when(z > hub)(lambda: signal(known.at[i + 1], at(z_down, y), chan))
 
+    to_half = hub - z
+
+    def to_later(part, source, d):
+        return pltpu.make_async_remote_copy(
+            source.at[pl.ds(MODES * part, MODES)],
+            ring_z.at[d - 1, pl.ds(MODES * part, MODES)],
+            z_send.at[part, d - 1],
+            z_recv.at[part, d - 1],
+            device_id=(at(lax.rem(z + d, zs), y), chan),
+            device_id_type=MESH,
+        )
+
+    def send_later(part, source, distances, among):
+        for d in distances:
+
+            @pl.when((z + d < zs) & among(d))
+            def _():
+                if part or d > 1:
+
+                    @pl.when(early)
+                    def _():
+                        pl.semaphore_wait(ready_z.at[d - 1], 1)
+
+                to_later(part, source, d).start()
+
+            pending.append(
+                functools.partial(
+                    pl.when((z + d < zs) & among(d)), to_later(part, source, d).wait_send
+                )
+            )
+
+    def in_half(d):
+        return (z >= hub) | (d < to_half)
+
+    for copy in row_copies:
+        copy.wait_recv()
+    total[MODES : MODES + 16, :] = info[ys - 1, MODES : MODES + 16, :]
+    send_later(1, total, (1,), lambda d: z < zs - 1)
+
     arrived(0, FACTOR, 0)
     send(3, FACTOR, 0)
     arrived(1, FACTOR, 1)
@@ -366,7 +416,6 @@
 
     for copy in y_copies:
         copy.wait_recv()
-    a384 = jnp.exp(-float(ROWS * (ys - 1)) * r)
     a512 = jnp.exp(-float(ROWS * ys) * r)
 
     def first_two(now, ends):
@@ -384,47 +433,26 @@
             heads[e, i : i + 1, :] = line
         return a127 * g0 + a126 * g1
 
-    firsts = info[0, MODES : MODES + 16, :].astype(F32)
-    ends = firsts
-    starts[0] = jnp.zeros_like(r)
-    start = info[0, 0:MODES, :].astype(F32)
-    for e in range(1, ys):
+    @pl.when(z == 0)
+    def _():
+        ends_before[...] = jnp.zeros_like(ends_before)
+
+    @pl.when(z > 0)
+    def _():
+        to_later(1, total, 1).wait_recv()
+        ends_before[...] = ring_z[0, MODES : MODES + 16, :].astype(F32)
+
+    ends = ends_before[...]
+    start = jnp.zeros_like(r)
+    for e in range(ys):
         now = info[e, MODES : MODES + 16, :].astype(F32)
         starts[e] = start
         start = start * a128 + (info[e, 0:MODES, :].astype(F32) + set_heads(e, now, ends))
         ends = now
     total[0:MODES, :] = start.astype(BF16)
-    line = lax.broadcasted_iota(jnp.int32, (16, width), 0)
-    rows_of_group = jnp.where((line & 3) < 2, firsts, ends)
-    total[MODES : MODES + 16, :] = rows_of_group.astype(BF16)
-
-    to_half = hub - z
-
-    def to_later(source, d):
-        return pltpu.make_async_remote_copy(
-            source, ring_z.at[d - 1], z_send.at[d - 1], z_recv.at[d - 1],
-            device_id=(at(lax.rem(z + d, zs), y), chan), device_id_type=MESH,
-        )
-
-    def send_sums(source, distances, which):
-        for d in distances:
-
-            @pl.when((z + d < zs) & which(d))
-            def _():
-                @pl.when(early)
-                def _():
-                    pl.semaphore_wait(ready_z.at[d - 1], 1)
-
-                to_later(source, d).start()
-
-            pending.append(
-                functools.partial(
-                    pl.when((z + d < zs) & which(d)), to_later(source, d).wait_send
-                )
-            )
-
-    send_sums(total, range(hub - 1, 0, -1), lambda d: (z >= hub) | (d < to_half))
-    send_sums(total, range(hub, 0, -1), lambda d: z == hub - 1)
+
+    send_later(0, total, range(hub - 1, 0, -1), in_half)
+    send_later(0, total, range(hub, 0, -1), lambda d: z == hub - 1)
 
     arrived(0, OWN, 0)
     send(3, OWN, 0)
@@ -437,32 +465,20 @@
     arrived(1, FACTOR, 0)
     send(6, FACTOR, 0)
     before[...] = jnp.zeros_like(before)
-    ends_before[...] = jnp.zeros_like(ends_before)
     for d in range(hub + 1, 0, -1):
 
         @pl.when((z >= d) & (early | (z - d >= hub - 2)))
         def _():
-            to_later(total, d).wait_recv()
-            now = ring_z[d - 1, MODES : MODES + 16, :].astype(F32)
-            g0, g1 = first_two(now, ends_before[...])
-            head = jnp.where(early | (z - d > hub - 2), 1.0, 0.0) * (a127 * g0 + a126 * g1)
-            arrived_sum = ring_z[d - 1, 0:MODES, :].astype(F32) + a384 * head
-            before[...] = before[...] * a512 + arrived_sum
-            ends_before[...] = now
-
-    head = set_heads(0, firsts, ends_before[...])
+            to_later(0, total, d).wait_recv()
+            before[...] = before[...] * a512 + ring_z[d - 1, 0:MODES, :].astype(F32)
 
     @pl.when(z == hub - 2)
     def _():
-        whole = total[0:MODES, :].astype(F32) + a384 * head + a512 * before[...]
-        half_sum[0:MODES, :] = whole.astype(BF16)
-        half_sum[MODES : MODES + 16, :] = total[MODES : MODES + 16, :]
-
-    send_sums(half_sum, range(hub + 1, 1, -1), lambda d: z == hub - 2)
+        half_sum[...] = (total[0:MODES, :].astype(F32) + a512 * before[...]).astype(BF16)
+
+    send_later(0, half_sum, range(hub + 1, 1, -1), lambda d: z == hub - 2)
 
     entering = starts[y] + jnp.exp(-float(ROWS) * y.astype(F32) * r) * before[...]
-    since = jnp.maximum(y - 1, 0).astype(F32)
-    entering = entering + jnp.where(y > 0, jnp.exp(-float(ROWS) * since * r) * head, 0.0)
     g0, g1, q126, q127 = (heads[y, i : i + 1, :] for i in range(4))
     later = entering + jnp.exp(r) * g0 + jnp.exp(2.0 * r) * g1
     rows = lax.broadcasted_iota(jnp.int32, (STEPS, LANES), 0)
@@ -593,17 +609,17 @@
         pltpu.VMEM((ys, 8, width), F32),
         pltpu.VMEM((ys, MODES, width), F32),
         pltpu.VMEM((MODES + 16, width), BF16),
-        pltpu.VMEM((MODES + 16, width), BF16),
+        pltpu.VMEM((MODES, width), BF16),
         pltpu.VMEM((zs - 1, MODES + 16, width), BF16),
         modes,
         pltpu.VMEM((CHIPS * CORES, STEPS, width), BF16),
         pltpu.VMEM((CHIPS * CORES, 2, PIECES, ROWS, width // PIECES), BF16),
         pltpu.VMEM((ROWS, width), F32),
         dma((10,)),
-        dma((ys - 1,)),
-        dma((ys - 1,)),
-        dma((zs - 1,)),
-        dma((zs - 1,)),
+        dma((2, ys - 1)),
+        dma((2, ys - 1)),
+        dma((2, zs - 1)),
+        dma((2, zs - 1)),
         dma((len(ROUTES), 2, PIECES)),
         dma((len(ROUTES), 2, PIECES)),
         dma((CHIPS * CORES,)),

time: 22.1 us -> 21.4 us (0.968)
  the two profiles are of different devices: /device:TPU:160 before, /device:TPU:225 now
where the time goes in v8:
time: 21.4 us; the launch traced here: 21.1 us
  Pallas kernels  20.4 us (95%)
  local copies, waits for them, and re-layouts  0.66 us (3%)
    pallas_call x1, Pallas kernels, per_device(): pl.pallas_call(functools.partial(kernel, zs, ys), out_shape=pltpu.VMEM((R...  20.4 us
    unnamed x1, local copies, waits for them, and re-layouts  0.66 us

profile of v8, /device:TPU:225, one launch (start us, length us, event | category | flops | bytes accessed | tf_op | source)
XLA Modules:
  0.0 21.1 jit_solution(15159398165865159763)
XLA Ops:
  0.0 20.4 %shard_map.100 = bf16[128,512]{1,0:T(8,128)(2,1)S(1)} custom-call(bf16[128,512]{1,0:T(8,128)(2,1)} %q_hbm.1, bf16[128,512]{1,0:T(8,128)(2,1)} %k_hbm.1, bf16[128,512]{1,0:T(8,128)(2,1)} %v_hbm.1, f32[3,3,512]{2,1,0:T(4,128)} %taps_hbm.1, f32[16,512]{1,0:T(8,128)} %bitcast.3, f32[16,512]{1,0:T(8,128)} %bitcast.4, f32[1,512]{1,0:T(1,128)} %bitcast.5, ...), custom_call_target="tpu_custom_call" | custom-call | tf_op jit(solution)/shard_map/pallas_call | solution.py:630
  20.4 0.7 %copy.12 = bf16[128,512]{1,0:T(8,128)(2,1)} copy(bf16[128,512]{1,0:T(8,128)(2,1)S(1)} %shard_map.100) | data formatting | bytes 262144

commit v9 on v8

--- a/solution.py
+++ b/solution.py
@@ -262,7 +262,7 @@
 
     def to_group(part):
         copies = []
-        for e in range(1, ys):
+        for e in sorted(range(1, ys), key=lambda e: -min(e, ys - e)):
             copy = pltpu.make_async_remote_copy(
                 info.at[y, pl.ds(MODES * part, MODES)],
                 info.at[y, pl.ds(MODES * part, MODES)],
@@ -500,7 +500,7 @@
         flow[0, :, cols] = values.astype(BF16)
 
     f_copies = {}
-    for ex in (2, 1, 3, 0):
+    for ex in (1, 3, 2, 0):
         for ec in range(CORES):
             slot = ex * CORES + ec
             if slot:

time: 21.4 us -> 20.9 us (0.977); the launches traced: 21.1 us -> 20.8 us
    pallas_call x1, Pallas kernels: 20.4 us -> 20.2 us  [per_device(): pl.pallas_call(functools.partial(kernel, zs, ys), out_shape=pltpu.VMEM((R...]
where the time goes in v9:
time: 20.9 us; the launch traced here: 20.8 us
  Pallas kernels  20.2 us (97%)
  local copies, waits for them, and re-layouts  0.66 us (3%)
    pallas_call x1, Pallas kernels, per_device(): pl.pallas_call(functools.partial(kernel, zs, ys), out_shape=pltpu.VMEM((R...  20.2 us
    unnamed x1, local copies, waits for them, and re-layouts  0.66 us

profile of v9, /device:TPU:225, one launch (start us, length us, event | category | flops | bytes accessed | tf_op | source)
XLA Modules:
  0.0 20.8 jit_solution(14019545394321075734)
XLA Ops:
  0.0 20.2 %shard_map.100 = bf16[128,512]{1,0:T(8,128)(2,1)S(1)} custom-call(bf16[128,512]{1,0:T(8,128)(2,1)} %q_hbm.1, bf16[128,512]{1,0:T(8,128)(2,1)} %k_hbm.1, bf16[128,512]{1,0:T(8,128)(2,1)} %v_hbm.1, f32[3,3,512]{2,1,0:T(4,128)} %taps_hbm.1, f32[16,512]{1,0:T(8,128)} %bitcast.3, f32[16,512]{1,0:T(8,128)} %bitcast.4, f32[1,512]{1,0:T(1,128)} %bitcast.5, ...), custom_call_target="tpu_custom_call" | custom-call | tf_op jit(solution)/shard_map/pallas_call | solution.py:630
  20.2 0.7 %copy.12 = bf16[128,512]{1,0:T(8,128)(2,1)} copy(bf16[128,512]{1,0:T(8,128)(2,1)S(1)} %shard_map.100) | data formatting | bytes 262144

commit v10 on v9

--- a/solution.py
+++ b/solution.py
@@ -138,7 +138,7 @@
             ]
         )
     ]
-    for i in (2, 5, 0, 1, 3, 4, 6, 7, 8, 9):
+    for i in (5, 3, 4, 2, 0, 1, 6, 7, 8, 9):
         loads[i].start()
     pending = []
 

time: 20.9 us -> 20.9 us (level)
  no operation moved by 1% of the time
where the time goes in v10:
time: 20.9 us; the launch traced here: 20.8 us
  Pallas kernels  20.2 us (97%)
  local copies, waits for them, and re-layouts  0.66 us (3%)
    pallas_call x1, Pallas kernels, per_device(): pl.pallas_call(functools.partial(kernel, zs, ys), out_shape=pltpu.VMEM((R...  20.2 us
    unnamed x1, local copies, waits for them, and re-layouts  0.66 us

profile of v10, /device:TPU:225, one launch (start us, length us, event | category | flops | bytes accessed | tf_op | source)
XLA Modules:
  0.0 20.8 jit_solution(17183067681987737680)
XLA Ops:
  0.0 20.2 %shard_map.100 = bf16[128,512]{1,0:T(8,128)(2,1)S(1)} custom-call(bf16[128,512]{1,0:T(8,128)(2,1)} %q_hbm.1, bf16[128,512]{1,0:T(8,128)(2,1)} %k_hbm.1, bf16[128,512]{1,0:T(8,128)(2,1)} %v_hbm.1, f32[3,3,512]{2,1,0:T(4,128)} %taps_hbm.1, f32[16,512]{1,0:T(8,128)} %bitcast.3, f32[16,512]{1,0:T(8,128)} %bitcast.4, f32[1,512]{1,0:T(1,128)} %bitcast.5, ...), custom_call_target="tpu_custom_call" | custom-call | tf_op jit(solution)/shard_map/pallas_call | solution.py:630
  20.2 0.7 %copy.12 = bf16[128,512]{1,0:T(8,128)(2,1)} copy(bf16[128,512]{1,0:T(8,128)(2,1)S(1)} %shard_map.100) | data formatting | bytes 262144
